TPU v7x, 256 devices: a whole 4x4x8 slice. The times are simulated.
256 devices in a mesh: row: 8 (over z_hi, core), col: 32 (over z_lo, x, y).
Axes of the slice: x: 4, y: 4, z: 8 (z_hi: 4, z_lo: 2; z = z_hi * 2 + z_lo), core: 2. Of those that a mesh axis runs over, the one named last changes fastest.
Arguments:
- amplitudes: float32 [512, 32768], P('row', 'col'), may hold values from -6 to 6
- integrals: float32 [256, 8, 128, 128], P('col'), may hold values from -0.1875 to 0.1875
- sources: int32 [256, 8], P('col'), may hold values from 0 to 255, as said below
- counts: int32 [256], P('col'), may hold values from 4 to 8, as said below
- tile_irrep: int32 [256], replicated, may hold values from 0 to 7, as said below
- partner: int32 [256], replicated, may hold values from 0 to 255, as said below
- occ_energy: float32 [512], P('row'), may hold values from -3 to -1
- virt_energy: float32 [32768], P('col'), may hold values from 1 to 5
Outputs:
- update: float32 [512, 32768], P('row', 'col')
Inputs may be any that keep to these rules, and one draw needn't show every extreme that they name: `sources`: each row lists 8 different tiles; in some rows one of them has another representation than the output tile, the others share it. `counts`: some tile has 8 counted sources. `tile_irrep`: each of the 8 representations labels exactly 32 tiles. An involution without fixed points that keeps the representation; partner[p] // 8 and p // 8 differ by 16.
All inputs are finite; a program needn't handle non-finite values.
Results may differ from a plain program's by a relative error of at most 0.0003.
Values sent between devices are 32-bit elements; how exact they have to be, the bound alone decides.
No kernel may reach another device: no remote copies, remote signals or barrier semaphores. Data moves between devices by JAX's collectives and lax.ppermute only.
A program may use at most 64 MiB of HBM per device.

v0:
```python
import jax
import jax.numpy as jnp
from jax import lax
from jax.sharding import PartitionSpec as P


def from_behind(shard, axis, by):
    length = lax.axis_size(axis)
    return lax.ppermute(shard, axis, [(i, (i + by) % length) for i in range(length)])


def shards(amplitudes, integrals, sources, counts, tile_irrep, partner, occ_energy, virt_energy):
    rows = amplitudes.shape[0]
    mine = integrals.shape[0]
    depth = integrals.shape[1]
    width = integrals.shape[-1]
    first = lax.axis_index("col") * mine
    half = lax.axis_size("row") // 2
    half_col = lax.axis_size("col") // 2
    my_irrep = lax.dynamic_slice_in_dim(tile_irrep, first, mine, 0)
    my_partner = lax.dynamic_slice_in_dim(partner, first, mine, 0)
    other_first = (lax.axis_index("col") + half_col) % lax.axis_size("col") * mine
    live = (jnp.arange(depth, dtype=jnp.int32)[None, :] < counts[:, None]) & (
        tile_irrep[sources] == my_irrep[:, None]
    )
    whole = lax.all_gather(amplitudes, "col", axis=1, tiled=True)
    whole = whole.reshape(rows, whole.shape[1] // width, width)

    def add_block(step, total):
        picked = whole[:, sources[:, step], :]
        active = lax.dynamic_index_in_dim(live, step, 1, keepdims=False)
        picked = jnp.where(active[None, :, None], picked, jnp.float32(0.0))
        blocks = lax.dynamic_index_in_dim(integrals, step, 1, keepdims=False)
        return total + jnp.einsum("omc,mce->ome", picked, blocks, precision=lax.Precision.HIGHEST)

    ladder = lax.fori_loop(
        0, jnp.max(counts), add_block, jnp.zeros((rows, mine, width), jnp.float32)
    )
    received = from_behind(ladder, "col", half_col)
    chosen = received[:, my_partner - other_first, :]
    mirrored = from_behind(chosen, "row", half)
    denom = occ_energy[:, None, None] - virt_energy.reshape(1, mine, width)
    update = (ladder + mirrored) / denom
    return update.reshape(rows, mine * width)


def solution(mesh):
    placed = (
        P("row", "col"),
        P("col", None, None, None),
        P("col", None),
        P("col"),
        P(),
        P(),
        P("row"),
        P("col"),
    )
    return jax.shard_map(
        shards, mesh=mesh, in_specs=placed, out_specs=P("row", "col"), check_vma=False
    )
```

profile of v0, /device:TPU:72, one launch (start us, length us, event | category | flops | bytes accessed | tf_op | source)
XLA Modules:
  0.0 267.6 jit_solution(17977177241940277402)
XLA Ops:
  9.6 1.5 gather_fusion.1
  11.1 1.3 reduce_max.9
  13.2 168.6 %all-gather.2.cloned.1.call-done = f32[64,32768]{1,0:T(8,128)} async-done(((f32[64,1024]{1,0:T(8,128)}), f32[64,32768]{1,0:T(8,128)}) %all-gather.2.cloned.1.call-update) | async-done | bytes 8388624 | tf_op jit(solution)/shard_map/all_gather | solution.py:26
  181.8 7.8 %copy_bitcast_fusion = f32[64,256,128]{2,0,1:T(8,128)} fusion(f32[64,32768]{1,0:T(8,128)} %all-gather.2.cloned.1.call-done), kind=kLoop, calls=%fused_computation.18 | loop fusion | bytes 16777216 | tf_op jit(solution)/shard_map/while | solution.py:36
  189.6 50.6 %while.10 = (s32[]{:T(128)}, f32[64,8,128]{2,0,1:T(8,128)S(1)}, s32[]{:T(128)}, f32[8,8,128,128]{3,2,1,0:T(8,128)}, pred[8,8]{0,1:T(8,128)(4,1)S(1)}, /*index=5*...) while((s32[]{:T(128)}, f32[64,8,128]{2,0,1:T(8,128)S(1)}, s32[]{:T(128)}, ...), condition=%wide.region_2.3_spmd, body=%wide.region_1.2_spmd.sunk | while | flops 100795424 | bytes 1839411 | solution.py:36
  190.3 3.9 %gather_fusion = f32[8,64,128]{2,1,0:T(8,128)S(1)} fusion(f32[64,256,128]{2,0,1:T(8,128)} %get-tuple-element.149, s32[1024]{0:T(1024)S(1)} %pad_clamp_fusion.4), kind=kCustom, calls=%fused_computation.clone.1 | custom fusion | bytes 524320 | tf_op jit(solution)/shard_map/while/body/gather | solution.py:30
  194.2 1.7 fusion.19
  196.5 3.9 %gather_fusion = f32[8,64,128]{2,1,0:T(8,128)S(1)} fusion(f32[64,256,128]{2,0,1:T(8,128)} %get-tuple-element.149, s32[1024]{0:T(1024)S(1)} %pad_clamp_fusion.4), kind=kCustom, calls=%fused_computation.clone.1 | custom fusion | bytes 524320 | tf_op jit(solution)/shard_map/while/body/gather | solution.py:30
  200.5 1.7 fusion.19
  202.8 3.9 %gather_fusion = f32[8,64,128]{2,1,0:T(8,128)S(1)} fusion(f32[64,256,128]{2,0,1:T(8,128)} %get-tuple-element.149, s32[1024]{0:T(1024)S(1)} %pad_clamp_fusion.4), kind=kCustom, calls=%fused_computation.clone.1 | custom fusion | bytes 524320 | tf_op jit(solution)/shard_map/while/body/gather | solution.py:30
  206.7 1.7 fusion.19
  209.0 3.9 %gather_fusion = f32[8,64,128]{2,1,0:T(8,128)S(1)} fusion(f32[64,256,128]{2,0,1:T(8,128)} %get-tuple-element.149, s32[1024]{0:T(1024)S(1)} %pad_clamp_fusion.4), kind=kCustom, calls=%fused_computation.clone.1 | custom fusion | bytes 524320 | tf_op jit(solution)/shard_map/while/body/gather | solution.py:30
  213.0 1.7 fusion.19
  215.3 3.9 %gather_fusion = f32[8,64,128]{2,1,0:T(8,128)S(1)} fusion(f32[64,256,128]{2,0,1:T(8,128)} %get-tuple-element.149, s32[1024]{0:T(1024)S(1)} %pad_clamp_fusion.4), kind=kCustom, calls=%fused_computation.clone.1 | custom fusion | bytes 524320 | tf_op jit(solution)/shard_map/while/body/gather | solution.py:30
  219.2 1.7 fusion.19
  221.6 3.9 %gather_fusion = f32[8,64,128]{2,1,0:T(8,128)S(1)} fusion(f32[64,256,128]{2,0,1:T(8,128)} %get-tuple-element.149, s32[1024]{0:T(1024)S(1)} %pad_clamp_fusion.4), kind=kCustom, calls=%fused_computation.clone.1 | custom fusion | bytes 524320 | tf_op jit(solution)/shard_map/while/body/gather | solution.py:30
  225.5 1.7 fusion.19
  227.8 3.9 %gather_fusion = f32[8,64,128]{2,1,0:T(8,128)S(1)} fusion(f32[64,256,128]{2,0,1:T(8,128)} %get-tuple-element.149, s32[1024]{0:T(1024)S(1)} %pad_clamp_fusion.4), kind=kCustom, calls=%fused_computation.clone.1 | custom fusion | bytes 524320 | tf_op jit(solution)/shard_map/while/body/gather | solution.py:30
  231.8 1.7 fusion.19
  234.1 3.9 %gather_fusion = f32[8,64,128]{2,1,0:T(8,128)S(1)} fusion(f32[64,256,128]{2,0,1:T(8,128)} %get-tuple-element.149, s32[1024]{0:T(1024)S(1)} %pad_clamp_fusion.4), kind=kCustom, calls=%fused_computation.clone.1 | custom fusion | bytes 524320 | tf_op jit(solution)/shard_map/while/body/gather | solution.py:30
  238.0 1.7 fusion.19
  240.8 5.9 %collective-permute-done = f32[64,8,128]{2,0,1:T(8,128)S(1)} collective-permute-done((f32[64,8,128]{2,0,1:T(8,128)S(1)}, f32[64,8,128]{2,0,1:T(8,128)S(1)}, u32[]{:S(2)}, u32[]{:S(2)}) %collective-permute-start) | collective-permute-done | bytes 262176 | tf_op jit(solution)/shard_map/ppermute | solution.py:9
  247.3 2.8 %collective-permute-start.1 = (f32[64,8,128]{2,0,1:T(8,128)S(1)}, f32[64,8,128]{2,0,1:T(8,128)S(1)}, u32[]{:S(2)}, u32[]{:S(2)}) collective-permute-start(f32[64,8,128]{2,0,1:T(8,128)S(1)} %bitcast.38), channel_id=1, source_target_pairs={{0,128},{32,160},{64,192},{96,224},{128,0},{160,32},{192,64},{224,... | collective-permute-start | bytes 786440 | tf_op jit(solution)/shard_map/ppermute | solution.py:9
  250.1 9.9 %collective-permute-done.1 = f32[64,8,128]{2,0,1:T(8,128)S(1)} collective-permute-done((f32[64,8,128]{2,0,1:T(8,128)S(1)}, f32[64,8,128]{2,0,1:T(8,128)S(1)}, u32[]{:S(2)}, u32[]{:S(2)}) %collective-permute-start.1) | collective-permute-done | bytes 262176 | tf_op jit(solution)/shard_map/ppermute | solution.py:9
  (46 shorter events, 6.0 us)
Async XLA Ops:
  6.5 175.3 %all-gather.2.cloned.1.call-start = ((), (), s32[]{:S(2)}) async-start(), calls=%async_computation | async-start | bytes 8650752 | tf_op jit(solution)/shard_map/all_gather | solution.py:26
  189.6 51.1 %copy-start.2 = (s32[256]{0:T(256)S(1)}, s32[256]{0:T(256)}, u32[]{:S(2)}) copy-start(s32[256]{0:T(256)} %param.15) | copy-start | bytes 3076
  189.6 70.3 %copy-start = (f32[1024]{0:T(1024)S(1)}, f32[1024]{0:T(1024)}, u32[]{:S(2)}) copy-start(f32[1024]{0:T(1024)} %param.17) | copy-start | bytes 12292
  189.6 70.3 %copy-start.1 = (f32[64]{0:T(128)S(1)}, f32[64]{0:T(128)}, u32[]{:S(2)}) copy-start(f32[64]{0:T(128)} %param.16) | copy-start | bytes 772
  240.3 6.5 %collective-permute-start = (f32[64,8,128]{2,0,1:T(8,128)S(1)}, f32[64,8,128]{2,0,1:T(8,128)S(1)}, u32[]{:S(2)}, u32[]{:S(2)}) collective-permute-start(f32[64,8,128]{2,0,1:T(8,128)S(1)} %get-tuple-element.43), channel_id=1, source_target_pairs={{0,16},{1,17},{2,18},{3,19},{4,20},{5,21},{6,22},{7,23},{8,24},{9,... | collective-permute-start | bytes 786440 | tf_op jit(solution)/shard_map/ppermute | solution.py:9
  247.3 12.6 %collective-permute-start.1 = (f32[64,8,128]{2,0,1:T(8,128)S(1)}, f32[64,8,128]{2,0,1:T(8,128)S(1)}, u32[]{:S(2)}, u32[]{:S(2)}) collective-permute-start(f32[64,8,128]{2,0,1:T(8,128)S(1)} %bitcast.38), channel_id=1, source_target_pairs={{0,128},{32,160},{64,192},{96,224},{128,0},{160,32},{192,64},{224,... | collective-permute-start | bytes 786440 | tf_op jit(solution)/shard_map/ppermute | solution.py:9
Sparse Core Ops, SparseCore 0:
  9.1 172.5 all-gather.1
where the time goes:
time: 269 us; the launch traced here: 268 us
  waiting for transfers between devices  185 us (69%)
  local copies, waits for them, and re-layouts  43.3 us (16%)
  matrix products  13.4 us (5%)
  between operations  13.4 us (5%)
  loops' own time  5.51 us (2%)
  other arithmetic  3.73 us (1%)
  starting transfers between devices  3.19 us (1%)
    all_gather x1, waiting for transfers between devices, shards(): whole = lax.all_gather(amplitudes, 'col', axis=1, tiled=True)  169 us
    gather x8, local copies, waits for them, and re-layouts, add_block(): picked = whole[:, sources[:, step], :]  31.6 us
    ppermute x2, waiting for transfers between devices, from_behind(): lax.ppermute(shard, axis, [(i, (i + by) % length) for i in range(length)])  15.8 us
    dot_general x8, matrix products, add_block(): jnp.einsum('omc,mce->ome', picked, blocks, precision=lax.Precision.HIGHEST)  13.4 us
    while x3, local copies, waits for them, and re-layouts, shards(): lax.fori_loop(0, jnp.max(counts), add_block, jnp.zeros((rows, mine, width...  8.64 us
    another operation x1, loops' own time, shards(): lax.fori_loop(0, jnp.max(counts), add_block, jnp.zeros((rows, mine, width...  5.51 us
  transfers between devices with their start and end apart: 3, of which 3 were waited for; matrix products, arithmetic and copies ran while one was open for 2% of the time, Pallas kernels for 0%

commit v1 on v0

v1 whole, which is shorter than its diff:
```python
import jax
import jax.numpy as jnp
from jax import lax
from jax.experimental import pallas as pl
from jax.experimental.pallas import tpu as pltpu
from jax.sharding import PartitionSpec as P

LANES = 128
SUB = 8
VMEM = pl.BlockSpec(memory_space=pltpu.VMEM)
SMEM = pl.BlockSpec(memory_space=pltpu.SMEM)


def halves(x):
    high = x.astype(jnp.bfloat16)
    low = (x - high.astype(jnp.float32)).astype(jnp.bfloat16)
    return high, low


def spread(groups, mine, depth, rows, tiles, src_ref, cnt_ref, irr_ref, amp_ref, out_ref):
    first = lax.axis_index("col") * mine
    share = rows // groups
    chunk = share * mine + SUB
    lane = lax.broadcasted_iota(jnp.int32, (SUB, LANES), 1)
    keys = jnp.full((SUB, LANES), -1, jnp.int32)
    for m in range(mine):
        base = irr_ref[first + m] * tiles
        count = cnt_ref[m]
        for k in range(depth):
            key = jnp.where(k < count, src_ref[m, k] + base, -1)
            keys = jnp.where(lane == m * depth + k, key, keys)
    keys = keys.astype(jnp.float32)
    for j in range(groups):
        out_ref[pl.ds(j * chunk + share * mine, SUB), :] = keys
    for i in range(rows // SUB):
        r, j = divmod(i * SUB, groups)
        for m in range(mine):
            out_ref[pl.ds(j * chunk + r * mine + m, SUB, stride=chunk), :] = amp_ref[
                pl.ds(i * SUB, SUB), pl.ds(m * LANES, LANES)
            ]


def pick(groups, mine, slots, share, tiles, irr_ref, got_ref, out_ref, hot_ref):
    chunk = share * mine + SUB
    table = jnp.concatenate(
        [
            jnp.concatenate(
                [got_ref[pl.ds(g * chunk + r * mine, mine), :] for g in range(groups)], axis=0
            )
            for r in range(share)
        ],
        axis=1,
    )
    high, low = halves(table)
    both = jnp.concatenate([high, low], axis=1)
    lists = got_ref[pl.ds(share * mine, groups, stride=chunk), :]
    lists = jnp.concatenate([lists, jnp.zeros((LANES - groups, LANES), jnp.float32)], axis=0)
    lists = lists.T
    tile = lax.broadcasted_iota(jnp.int32, (1, tiles), 1)
    label = (irr_ref[...] * tiles + tile).astype(jnp.float32)
    for g in range(groups):
        hot = lists[:slots, g : g + 1] == label
        hot_ref[pl.ds(g * slots, slots), :] = jnp.where(hot, 1.0, 0.0).astype(jnp.bfloat16)
    width = share * LANES
    step = 512
    for b in range(groups * slots // step):
        sums = jnp.dot(
            hot_ref[pl.ds(b * step, step), :], both, preferred_element_type=jnp.float32
        )
        sums = sums[:, :width] + sums[:, width:]
        for g in range(step // slots):
            for r in range(share):
                to = ((b * step // slots + g) * share + r) * slots
                out_ref[pl.ds(to, slots), :] = sums[
                    g * slots : (g + 1) * slots, r * LANES : (r + 1) * LANES
                ]


def multiply(groups, mine, depth, rows, got_ref, int_ref, out_ref):
    slots = mine * depth
    share = rows // groups
    for m in range(mine):
        cols = []
        for k in range(depth):
            cols.append(
                jnp.concatenate(
                    [
                        got_ref[pl.ds(r * slots + m * depth + k, groups, stride=share * slots), :]
                        for r in range(share)
                    ],
                    axis=0,
                )
            )
        left_high, left_low = halves(jnp.concatenate(cols, axis=1))
        right_high, right_low = halves(int_ref[pl.ds(m * depth * LANES, depth * LANES), :])
        sums = jnp.dot(
            jnp.concatenate([left_high, left_low], axis=0),
            jnp.concatenate([right_high, right_low], axis=1),
            preferred_element_type=jnp.float32,
        )
        sums = sums[:, :LANES] + sums[:, LANES:]
        out_ref[m] = sums[:rows] + sums[rows:]


def finish(mine, rows, half_col, cols, par_ref, lad_ref, mir_ref, occ_ref, virt_ref, out_ref):
    me = lax.axis_index("col")
    other_first = lax.rem(me + half_col, cols) * mine
    row = lax.broadcasted_iota(jnp.int32, (rows, rows), 0)
    col = lax.broadcasted_iota(jnp.int32, (rows, rows), 1)
    occ = jnp.sum(jnp.where(row == col, occ_ref[...], 0.0), axis=1, keepdims=True)
    for m in range(mine):
        at = par_ref[me * mine + m] - other_first
        lanes = pl.ds(m * LANES, LANES)
        out_ref[:, lanes] = (lad_ref[m] + mir_ref[at]) / (occ - virt_ref[:, lanes])


def shards(amplitudes, integrals, sources, counts, tile_irrep, partner, occ_energy, virt_energy):
    rows = amplitudes.shape[0]
    mine, depth, width, _ = integrals.shape
    tiles = tile_irrep.shape[0]
    cols = lax.axis_size("col")
    heights = lax.axis_size("row")
    slots = mine * depth
    share = rows // cols
    chunk = share * mine + SUB
    f32 = jnp.float32

    def call(body, out, *args, specs, scratch=(), flops=0, moved=0):
        return pl.pallas_call(
            body,
            out_shape=jax.ShapeDtypeStruct(out, f32),
            in_specs=specs,
            out_specs=VMEM,
            scratch_shapes=scratch,
            compiler_params=pltpu.CompilerParams(vmem_limit_bytes=40 * 1024 * 1024),
            cost_estimate=pl.CostEstimate(flops=flops, bytes_accessed=moved, transcendentals=0),
        )(*args)

    sent = call(
        lambda *refs: spread(cols, mine, depth, rows, tiles, *refs),
        (cols * chunk, LANES),
        sources, counts, tile_irrep, amplitudes,
        specs=[SMEM, SMEM, SMEM, VMEM],
        moved=2 * amplitudes.size * 4,
    )
    got = lax.all_to_all(sent.reshape(cols, chunk, LANES), "col", 0, 0)
    sent = call(
        lambda *refs: pick(cols, mine, slots, share, tiles, *refs),
        (cols * share * slots, LANES),
        tile_irrep.reshape(1, tiles), got.reshape(cols * chunk, LANES),
        specs=[VMEM, VMEM],
        scratch=[pltpu.VMEM((cols * slots, tiles), jnp.bfloat16)],
        flops=4 * cols * slots * tiles * share * LANES,
        moved=cols * slots * share * LANES * 4,
    )
    got = lax.all_to_all(sent.reshape(cols, share * slots, LANES), "col", 0, 0)
    ladder = call(
        lambda *refs: multiply(cols, mine, depth, rows, *refs),
        (mine, rows, width),
        got.reshape(cols * share * slots, LANES),
        integrals.reshape(mine * depth * width, width),
        specs=[VMEM, VMEM],
        flops=8 * rows * mine * depth * width * width,
        moved=integrals.size * 4 + got.size * 4,
    )
    pairs = [
        (r * cols + c, (r + heights // 2) % heights * cols + (c + cols // 2) % cols)
        for r in range(heights)
        for c in range(cols)
    ]
    mirrored = lax.ppermute(ladder, ("row", "col"), pairs)
    return call(
        lambda *refs: finish(mine, rows, cols // 2, cols, *refs),
        (rows, mine * width),
        partner, ladder, mirrored, occ_energy.reshape(1, rows), virt_energy.reshape(1, mine * width),
        specs=[SMEM, VMEM, VMEM, VMEM, VMEM],
        moved=4 * rows * mine * width * 3,
    )


def solution(mesh):
    placed = (
        P("row", "col"),
        P("col", None, None, None),
        P("col", None),
        P("col"),
        P(),
        P(),
        P("row"),
        P("col"),
    )
    return jax.shard_map(
        shards, mesh=mesh, in_specs=placed, out_specs=P("row", "col"), check_vma=False
    )
```

time: 269 us -> 73.4 us (0.27)
  the two profiles are of different devices: /device:TPU:72 before, /device:TPU:2 now
where the time goes in v1:
time: 73.4 us; the launch traced here: 73.2 us
  blocking collectives  48.8 us (66%)
  waiting for transfers between devices  9.67 us (13%)
  starting transfers between devices  6.36 us (9%)
  Pallas kernels  4.67 us (6%)
  local copies, waits for them, and re-layouts  3.67 us (5%)
    all_to_all x1, blocking collectives, shards(): got = lax.all_to_all(sent.reshape(cols, share * slots, LANES), 'col', 0, 0)  30.9 us
    all_to_all x1, blocking collectives, shards(): got = lax.all_to_all(sent.reshape(cols, chunk, LANES), 'col', 0, 0)  17.8 us
    ppermute x1, waiting for transfers between devices, shards(): mirrored = lax.ppermute(ladder, ('row', 'col'), pairs)  9.67 us
    ppermute x1, starting transfers between devices, shards(): mirrored = lax.ppermute(ladder, ('row', 'col'), pairs)  6.36 us
    pallas_call x4, Pallas kernels, call(): pl.pallas_call(body, out_shape=jax.ShapeDtypeStruct(out, f32), in_specs=s...  4.67 us
    unnamed x18, local copies, waits for them, and re-layouts  3.67 us
  transfers between devices with their start and end apart: 1, of which 1 were waited for; matrix products, arithmetic and copies ran while one was open for 0% of the time, Pallas kernels for 0%

profile of v1, /device:TPU:2, one launch (start us, length us, event | category | flops | bytes accessed | tf_op | source)
XLA Modules:
  0.0 73.2 jit_solution(973659847887191129)
XLA Ops:
  0.0 0.0 copy-start.1
  0.0 0.9 %copy-done.1 = f32[64,1024]{1,0:T(8,128)S(1)} copy-done((f32[64,1024]{1,0:T(8,128)S(1)}, f32[64,1024]{1,0:T(8,128)}, u32[]{:S(2)}) %copy-start.1) | copy-done | bytes 262168
  1.0 0.0 copy-start.2
  1.0 0.7 copy-done.2
  1.6 0.0 copy-start.4
  1.6 0.7 copy-done.4
  2.3 0.0 copy-start.7
  2.3 0.7 copy-done.7
  3.0 0.7 shard_map.82
  3.7 17.8 %all_to_all.10 = f32[32,24,128]{2,1,0:T(8,128)S(1)} all-to-all(f32[32,24,128]{2,1,0:T(8,128)S(1)} %bitcast.12), channel_id=1, replica_groups=mesh['row'=8,'col'=32] {'col'}, dimensions={0} | all-to-all | bytes 786432 | tf_op jit(solution)/shard_map/all_to_all | solution.py:146
  21.6 0.0 copy-start.5
  21.6 0.7 copy-done.5
  22.2 0.9 %shard_map.83 = f32[4096,128]{1,0:T(8,128)S(1)} custom-call(s32[1,256]{1,0:T(1,128)S(1)} %bitcast.14, f32[768,128]{1,0:T(8,128)S(1)} %bitcast.11), custom_call_target="tpu_custom_call" | custom-call | flops 536870912 | bytes 2097152 | tf_op jit(solution)/shard_map/pallas_call | solution.py:129
  23.1 0.0 copy-start
  23.2 30.9 %all_to_all.11 = f32[32,128,128]{2,1,0:T(8,128)S(1)} all-to-all(f32[32,128,128]{2,1,0:T(8,128)S(1)} %bitcast.9), channel_id=1, replica_groups=mesh['row'=8,'col'=32] {'col'}, dimensions={0} | all-to-all | bytes 4194304 | tf_op jit(solution)/shard_map/all_to_all | solution.py:156
  54.1 0.0 copy-done
  54.1 0.0 copy-start.3
  54.1 1.7 %shard_map.84.refs_1_ = f32[8,64,128]{2,1,0:T(8,128)S(1)} custom-call(f32[4096,128]{1,0:T(8,128)S(1)} %bitcast.8, f32[8192,128]{1,0:T(8,128)S(1)} %bitcast.10), custom_call_target="tpu_custom_call" | custom-call | flops 536870912 | bytes 6291456 | tf_op jit(solution)/shard_map/pallas_call | solution.py:129
  55.7 6.4 %collective-permute-start = (f32[8,64,128]{2,1,0:T(8,128)S(1)}, f32[8,64,128]{2,1,0:T(8,128)S(1)}, u32[]{:S(2)}, u32[]{:S(2)}) collective-permute-start(f32[8,64,128]{2,1,0:T(8,128)S(1)} %shard_map.84.refs_1_), channel_id=1, source_target_pairs={{0,144},{1,145},{2,146},{3,147},{4,148},{5,149},{6,150},{7,151},{8... | collective-permute-start | bytes 786440 | tf_op jit(solution)/shard_map/ppermute | solution.py:171
  62.1 9.7 %collective-permute-done.refs_2_ = f32[8,64,128]{2,1,0:T(8,128)S(1)} collective-permute-done((f32[8,64,128]{2,1,0:T(8,128)S(1)}, f32[8,64,128]{2,1,0:T(8,128)S(1)}, u32[]{:S(2)}, u32[]{:S(2)}) %collective-permute-start) | collective-permute-done | bytes 262176 | tf_op jit(solution)/shard_map/ppermute | solution.py:171
  71.8 0.0 copy-done.3
  71.8 0.0 copy-done.6
  71.8 0.0 copy-done.8
  71.8 1.4 %shard_map.85 = f32[64,1024]{1,0:T(8,128)} custom-call(s32[256]{0:T(256)S(1)} %copy-done.6, f32[8,64,128]{2,1,0:T(8,128)S(1)} %shard_map.84.refs_1_, f32[8,64,128]{2,1,0:T(8,128)S(1)} %collective-permute-done.refs_2_, f32[1,64]{1,0:T(1,128)S(1)} %bitcast.15, f32[1,1024]{1,0:T(1,128)S(1)} %bitcast.13), custom_call_target="tpu_custom_call" | custom-call | bytes 786432 | tf_op jit(solution)/shard_map/pallas_call | solution.py:129
  (2 shorter events, 0.0 us)
Async XLA Ops:
  0.0 0.9 %copy-start.1 = (f32[64,1024]{1,0:T(8,128)S(1)}, f32[64,1024]{1,0:T(8,128)}, u32[]{:S(2)}) copy-start(f32[64,1024]{1,0:T(8,128)} %refs_3_.1) | copy-start | bytes 786436
  1.0 0.7 copy-start.2
  1.6 0.7 copy-start.4
  2.3 0.7 copy-start.7
  21.6 0.7 copy-start.5
  23.1 30.9 %copy-start = (f32[8,8,128,128]{3,2,1,0:T(8,128)S(1)}, f32[8,8,128,128]{3,2,1,0:T(8,128)}, u32[]{:S(2)}) copy-start(f32[8,8,128,128]{3,2,1,0:T(8,128)} %param.9) | copy-start | bytes 12582916
  54.1 17.7 %copy-start.3 = (f32[1024]{0:T(1024)S(1)}, f32[1024]{0:T(1024)}, u32[]{:S(2)}) copy-start(f32[1024]{0:T(1024)} %param.15) | copy-start | bytes 12292
  54.1 17.7 %copy-start.6 = (s32[256]{0:T(256)S(1)}, s32[256]{0:T(256)}, u32[]{:S(2)}) copy-start(s32[256]{0:T(256)} %refs_0_.3) | copy-start | bytes 3076
  54.1 17.7 %copy-start.8 = (f32[64]{0:T(128)S(1)}, f32[64]{0:T(128)}, u32[]{:S(2)}) copy-start(f32[64]{0:T(128)} %param.14) | copy-start | bytes 772
  55.7 16.0 %collective-permute-start = (f32[8,64,128]{2,1,0:T(8,128)S(1)}, f32[8,64,128]{2,1,0:T(8,128)S(1)}, u32[]{:S(2)}, u32[]{:S(2)}) collective-permute-start(f32[8,64,128]{2,1,0:T(8,128)S(1)} %shard_map.84.refs_1_), channel_id=1, source_target_pairs={{0,144},{1,145},{2,146},{3,147},{4,148},{5,149},{6,150},{7,151},{8... | collective-permute-start | bytes 786440 | tf_op jit(solution)/shard_map/ppermute | solution.py:171

commit v2 on v1

--- a/solution.py
+++ b/solution.py
@@ -8,7 +8,7 @@
 LANES = 128
 SUB = 8
 VMEM = pl.BlockSpec(memory_space=pltpu.VMEM)
-SMEM = pl.BlockSpec(memory_space=pltpu.SMEM)
+HBM = pl.BlockSpec(memory_space=pltpu.HBM)
 
 
 def halves(x):
@@ -17,10 +17,23 @@
     return high, low
 
 
-def spread(groups, mine, depth, rows, tiles, src_ref, cnt_ref, irr_ref, amp_ref, out_ref):
+def spread(
+    groups, mine, depth, rows, tiles,
+    src_hbm, cnt_hbm, irr_hbm, row_hbm, amp_hbm, out_ref,
+    src_ref, cnt_ref, irr_ref, row_ref, amp_ref, sems,
+):
+    pairs = [
+        (amp_hbm, amp_ref), (irr_hbm, irr_ref), (src_hbm, src_ref), (cnt_hbm, cnt_ref),
+        (row_hbm, row_ref),
+    ]
+    copies = [pltpu.make_async_copy(a, b, sems.at[n]) for n, (a, b) in enumerate(pairs)]
+    for copy in copies:
+        copy.start()
     first = lax.axis_index("col") * mine
     share = rows // groups
     chunk = share * mine + SUB
+    for copy in copies[1:]:
+        copy.wait()
     lane = lax.broadcasted_iota(jnp.int32, (SUB, LANES), 1)
     keys = jnp.full((SUB, LANES), -1, jnp.int32)
     for m in range(mine):
@@ -29,9 +42,14 @@
         for k in range(depth):
             key = jnp.where(k < count, src_ref[m, k] + base, -1)
             keys = jnp.where(lane == m * depth + k, key, keys)
+    line = lax.broadcasted_iota(jnp.int32, (SUB, LANES), 0)
+    for n in range(tiles // LANES):
+        label = row_ref[:, pl.ds(n * LANES, LANES)] * tiles + n * LANES
+        keys = jnp.where(line == n + 1, label + lane, keys)
     keys = keys.astype(jnp.float32)
     for j in range(groups):
         out_ref[pl.ds(j * chunk + share * mine, SUB), :] = keys
+    copies[0].wait()
     for i in range(rows // SUB):
         r, j = divmod(i * SUB, groups)
         for m in range(mine):
@@ -40,7 +58,7 @@
             ]
 
 
-def pick(groups, mine, slots, share, tiles, irr_ref, got_ref, out_ref, hot_ref):
+def pick(groups, mine, slots, share, tiles, got_ref, out_ref, hot_ref):
     chunk = share * mine + SUB
     table = jnp.concatenate(
         [
@@ -56,8 +74,9 @@
     lists = got_ref[pl.ds(share * mine, groups, stride=chunk), :]
     lists = jnp.concatenate([lists, jnp.zeros((LANES - groups, LANES), jnp.float32)], axis=0)
     lists = lists.T
-    tile = lax.broadcasted_iota(jnp.int32, (1, tiles), 1)
-    label = (irr_ref[...] * tiles + tile).astype(jnp.float32)
+    label = jnp.concatenate(
+        [got_ref[pl.ds(share * mine + 1 + n, 1), :] for n in range(tiles // LANES)], axis=1
+    )
     for g in range(groups):
         hot = lists[:slots, g : g + 1] == label
         hot_ref[pl.ds(g * slots, slots), :] = jnp.where(hot, 1.0, 0.0).astype(jnp.bfloat16)
@@ -76,9 +95,15 @@
                 ]
 
 
-def multiply(groups, mine, depth, rows, got_ref, int_ref, out_ref):
+def multiply(
+    groups, half, mine, depth, rows, par_hbm, got_ref, int_ref, out_ref, turned_ref, par_ref, sem
+):
+    copy = pltpu.make_async_copy(par_hbm, par_ref, sem)
+    copy.start()
     slots = mine * depth
     share = rows // groups
+    me = lax.axis_index("col")
+    other_first = lax.rem(me + half, groups) * mine
     for m in range(mine):
         cols = []
         for k in range(depth):
@@ -99,19 +124,20 @@
             preferred_element_type=jnp.float32,
         )
         sums = sums[:, :LANES] + sums[:, LANES:]
-        out_ref[m] = sums[:rows] + sums[rows:]
-
-
-def finish(mine, rows, half_col, cols, par_ref, lad_ref, mir_ref, occ_ref, virt_ref, out_ref):
-    me = lax.axis_index("col")
-    other_first = lax.rem(me + half_col, cols) * mine
+        sums = sums[:rows] + sums[rows:]
+        out_ref[m] = sums
+        if m == 0:
+            copy.wait()
+        turned_ref[par_ref[me * mine + m] - other_first] = sums
+
+
+def finish(mine, rows, lad_ref, mir_ref, occ_ref, virt_ref, out_ref):
     row = lax.broadcasted_iota(jnp.int32, (rows, rows), 0)
     col = lax.broadcasted_iota(jnp.int32, (rows, rows), 1)
     occ = jnp.sum(jnp.where(row == col, occ_ref[...], 0.0), axis=1, keepdims=True)
     for m in range(mine):
-        at = par_ref[me * mine + m] - other_first
         lanes = pl.ds(m * LANES, LANES)
-        out_ref[:, lanes] = (lad_ref[m] + mir_ref[at]) / (occ - virt_ref[:, lanes])
+        out_ref[:, lanes] = (lad_ref[m] + mir_ref[m]) / (occ - virt_ref[:, lanes])
 
 
 def shards(amplitudes, integrals, sources, counts, tile_irrep, partner, occ_energy, virt_energy):
@@ -125,41 +151,52 @@
     chunk = share * mine + SUB
     f32 = jnp.float32
 
-    def call(body, out, *args, specs, scratch=(), flops=0, moved=0):
+    def call(body, out, *args, specs, scratch=(), flops=0, moved=0, room=40):
         return pl.pallas_call(
             body,
-            out_shape=jax.ShapeDtypeStruct(out, f32),
+            out_shape=[jax.ShapeDtypeStruct(shape, f32) for shape in out],
             in_specs=specs,
-            out_specs=VMEM,
+            out_specs=[VMEM] * len(out),
             scratch_shapes=scratch,
-            compiler_params=pltpu.CompilerParams(vmem_limit_bytes=40 * 1024 * 1024),
+            compiler_params=pltpu.CompilerParams(vmem_limit_bytes=room * 1024 * 1024),
             cost_estimate=pl.CostEstimate(flops=flops, bytes_accessed=moved, transcendentals=0),
         )(*args)
 
-    sent = call(
+    (sent,) = call(
         lambda *refs: spread(cols, mine, depth, rows, tiles, *refs),
-        (cols * chunk, LANES),
-        sources, counts, tile_irrep, amplitudes,
-        specs=[SMEM, SMEM, SMEM, VMEM],
+        [(cols * chunk, LANES)],
+        sources, counts, tile_irrep, tile_irrep.reshape(1, tiles), amplitudes,
+        specs=[HBM] * 5,
+        scratch=[
+            pltpu.SMEM(sources.shape, jnp.int32),
+            pltpu.SMEM(counts.shape, jnp.int32),
+            pltpu.SMEM((tiles,), jnp.int32),
+            pltpu.VMEM((1, tiles), jnp.int32),
+            pltpu.VMEM(amplitudes.shape, f32),
+            pltpu.SemaphoreType.DMA((5,)),
+        ],
         moved=2 * amplitudes.size * 4,
+        room=63,
     )
     got = lax.all_to_all(sent.reshape(cols, chunk, LANES), "col", 0, 0)
-    sent = call(
+    (sent,) = call(
         lambda *refs: pick(cols, mine, slots, share, tiles, *refs),
-        (cols * share * slots, LANES),
-        tile_irrep.reshape(1, tiles), got.reshape(cols * chunk, LANES),
-        specs=[VMEM, VMEM],
+        [(cols * share * slots, LANES)],
+        got.reshape(cols * chunk, LANES),
+        specs=[VMEM],
         scratch=[pltpu.VMEM((cols * slots, tiles), jnp.bfloat16)],
         flops=4 * cols * slots * tiles * share * LANES,
         moved=cols * slots * share * LANES * 4,
     )
     got = lax.all_to_all(sent.reshape(cols, share * slots, LANES), "col", 0, 0)
-    ladder = call(
-        lambda *refs: multiply(cols, mine, depth, rows, *refs),
-        (mine, rows, width),
+    ladder, turned = call(
+        lambda *refs: multiply(cols, cols // 2, mine, depth, rows, *refs),
+        [(mine, rows, width)] * 2,
+        partner,
         got.reshape(cols * share * slots, LANES),
         integrals.reshape(mine * depth * width, width),
-        specs=[VMEM, VMEM],
+        specs=[HBM, VMEM, VMEM],
+        scratch=[pltpu.SMEM((tiles,), jnp.int32), pltpu.SemaphoreType.DMA],
         flops=8 * rows * mine * depth * width * width,
         moved=integrals.size * 4 + got.size * 4,
     )
@@ -168,14 +205,15 @@
         for r in range(heights)
         for c in range(cols)
     ]
-    mirrored = lax.ppermute(ladder, ("row", "col"), pairs)
-    return call(
-        lambda *refs: finish(mine, rows, cols // 2, cols, *refs),
-        (rows, mine * width),
-        partner, ladder, mirrored, occ_energy.reshape(1, rows), virt_energy.reshape(1, mine * width),
-        specs=[SMEM, VMEM, VMEM, VMEM, VMEM],
+    mirrored = lax.ppermute(turned, ("row", "col"), pairs)
+    (update,) = call(
+        lambda *refs: finish(mine, rows, *refs),
+        [(rows, mine * width)],
+        ladder, mirrored, occ_energy.reshape(1, rows), virt_energy.reshape(1, mine * width),
+        specs=[VMEM] * 4,
         moved=4 * rows * mine * width * 3,
     )
+    return update
 
 
 def solution(mesh):

time: 73.4 us -> 70.8 us (0.965)
  local copies, waits for them, and re-layouts: 3.67 us -> 0.02 us
  Pallas kernels: 4.67 us -> 5.47 us
    unnamed x18 -> x8, local copies, waits for them, and re-layouts: 3.67 us -> 0.02 us
    pallas_call x4, Pallas kernels: 4.67 us -> 5.47 us  [call(): pl.pallas_call(body, out_shape=[jax.ShapeDtypeStruct(shape, f32) for shap...]
where the time goes in v2:
time: 70.8 us; the launch traced here: 70.5 us
  blocking collectives  49 us (69%)
  waiting for transfers between devices  9.67 us (14%)
  starting transfers between devices  6.36 us (9%)
  Pallas kernels  5.47 us (8%)
    all_to_all x1, blocking collectives, shards(): got = lax.all_to_all(sent.reshape(cols, share * slots, LANES), 'col', 0, 0)  30.9 us
    all_to_all x1, blocking collectives, shards(): got = lax.all_to_all(sent.reshape(cols, chunk, LANES), 'col', 0, 0)  18.1 us
    ppermute x1, waiting for transfers between devices, shards(): mirrored = lax.ppermute(turned, ('row', 'col'), pairs)  9.67 us
    ppermute x1, starting transfers between devices, shards(): mirrored = lax.ppermute(turned, ('row', 'col'), pairs)  6.36 us
    pallas_call x4, Pallas kernels, call(): pl.pallas_call(body, out_shape=[jax.ShapeDtypeStruct(shape, f32) for shap...  5.47 us
  transfers between devices with their start and end apart: 1, of which 1 were waited for; matrix products, arithmetic and copies ran while one was open for 0% of the time, Pallas kernels for 0%

profile of v2, /device:TPU:2, one launch (start us, length us, event | category | flops | bytes accessed | tf_op | source)
XLA Modules:
  0.0 70.5 jit_solution(11699229812716190951)
XLA Ops:
  0.0 1.8 %shard_map.82 = f32[768,128]{1,0:T(8,128)} custom-call(s32[8,8]{1,0:T(8,128)} %refs_0_.2, s32[8]{0:T(128)} %refs_1_.1, s32[256]{0:T(256)} %refs_2_.1, s32[1,256]{1,0:T(1,128)} %bitcast.15, f32[64,1024]{1,0:T(8,128)} %refs_4_.1), custom_call_target="tpu_custom_call" | custom-call | bytes 524288 | tf_op jit(solution)/shard_map/pallas_call | solution.py:155
  1.8 18.1 %all_to_all.10 = f32[32,24,128]{2,1,0:T(8,128)S(1)} all-to-all(f32[32,24,128]{2,1,0:T(8,128)} %bitcast.14), channel_id=1, replica_groups=mesh['row'=8,'col'=32] {'col'}, dimensions={0} | all-to-all | bytes 786432 | tf_op jit(solution)/shard_map/all_to_all | solution.py:181
  19.9 0.9 %shard_map.83 = f32[4096,128]{1,0:T(8,128)S(1)} custom-call(f32[768,128]{1,0:T(8,128)S(1)} %bitcast.11), custom_call_target="tpu_custom_call" | custom-call | flops 536870912 | bytes 2097152 | tf_op jit(solution)/shard_map/pallas_call | solution.py:155
  20.8 0.0 copy-start
  20.8 0.0 copy-start.2
  20.8 30.9 %all_to_all.11 = f32[32,128,128]{2,1,0:T(8,128)S(1)} all-to-all(f32[32,128,128]{2,1,0:T(8,128)S(1)} %bitcast.9), channel_id=1, replica_groups=mesh['row'=8,'col'=32] {'col'}, dimensions={0} | all-to-all | bytes 4194304 | tf_op jit(solution)/shard_map/all_to_all | solution.py:191
  51.7 0.0 copy-done
  51.7 0.0 copy-done.2
  51.7 0.0 copy-start.1
  51.7 0.0 copy-start.3
  51.7 2.0 %shard_map.84 = (f32[8,64,128]{2,1,0:T(8,128)S(1)}, f32[8,64,128]{2,1,0:T(8,128)S(1)}) custom-call(s32[256]{0:T(256)S(1)} %copy-done.2, f32[4096,128]{1,0:T(8,128)S(1)} %bitcast.8, f32[8192,128]{1,0:T(8,128)S(1)} %bitcast.10), custom_call_target="tpu_custom_call" | custom-call | flops 536870912 | bytes 6291456 | tf_op jit(solution)/shard_map/pallas_call | solution.py:155
  53.7 6.4 %collective-permute-start = (f32[8,64,128]{2,1,0:T(8,128)S(1)}, f32[8,64,128]{2,1,0:T(8,128)S(1)}, u32[]{:S(2)}, u32[]{:S(2)}) collective-permute-start(f32[8,64,128]{2,1,0:T(8,128)S(1)} %get-tuple-element.8), channel_id=1, source_target_pairs={{0,144},{1,145},{2,146},{3,147},{4,148},{5,149},{6,150},{7,151},{8... | collective-permute-start | bytes 786440 | tf_op jit(solution)/shard_map/ppermute | solution.py:208
  60.0 9.7 %collective-permute-done.refs_1_ = f32[8,64,128]{2,1,0:T(8,128)S(1)} collective-permute-done((f32[8,64,128]{2,1,0:T(8,128)S(1)}, f32[8,64,128]{2,1,0:T(8,128)S(1)}, u32[]{:S(2)}, u32[]{:S(2)}) %collective-permute-start) | collective-permute-done | bytes 262176 | tf_op jit(solution)/shard_map/ppermute | solution.py:208
  69.7 0.0 copy-done.1
  69.7 0.0 copy-done.3
  69.7 0.8 %shard_map.85 = f32[64,1024]{1,0:T(8,128)} custom-call(f32[8,64,128]{2,1,0:T(8,128)S(1)} %get-tuple-element.7.refs_0_, f32[8,64,128]{2,1,0:T(8,128)S(1)} %collective-permute-done.refs_1_, f32[1,64]{1,0:T(1,128)S(1)} %bitcast.13, f32[1,1024]{1,0:T(1,128)S(1)} %bitcast.12), custom_call_target="tpu_custom_call" | custom-call | bytes 786432 | tf_op jit(solution)/shard_map/pallas_call | solution.py:155
Async XLA Ops:
  20.8 30.9 %copy-start = (f32[8,8,128,128]{3,2,1,0:T(8,128)S(1)}, f32[8,8,128,128]{3,2,1,0:T(8,128)}, u32[]{:S(2)}) copy-start(f32[8,8,128,128]{3,2,1,0:T(8,128)} %param.9) | copy-start | bytes 12582916
  20.8 30.9 %copy-start.2 = (s32[256]{0:T(256)S(1)}, s32[256]{0:T(256)}, u32[]{:S(2)}) copy-start(s32[256]{0:T(256)} %refs_0_.3) | copy-start | bytes 3076
  51.7 18.0 %copy-start.1 = (f32[1024]{0:T(1024)S(1)}, f32[1024]{0:T(1024)}, u32[]{:S(2)}) copy-start(f32[1024]{0:T(1024)} %param.15) | copy-start | bytes 12292
  51.7 18.0 %copy-start.3 = (f32[64]{0:T(128)S(1)}, f32[64]{0:T(128)}, u32[]{:S(2)}) copy-start(f32[64]{0:T(128)} %param.14) | copy-start | bytes 772
  53.7 16.0 %collective-permute-start = (f32[8,64,128]{2,1,0:T(8,128)S(1)}, f32[8,64,128]{2,1,0:T(8,128)S(1)}, u32[]{:S(2)}, u32[]{:S(2)}) collective-permute-start(f32[8,64,128]{2,1,0:T(8,128)S(1)} %get-tuple-element.8), channel_id=1, source_target_pairs={{0,144},{1,145},{2,146},{3,147},{4,148},{5,149},{6,150},{7,151},{8... | collective-permute-start | bytes 786440 | tf_op jit(solution)/shard_map/ppermute | solution.py:208

commit v3 on v2

v3 whole, which is shorter than its diff:
```python
import jax
import jax.numpy as jnp
from jax import lax
from jax.experimental import pallas as pl
from jax.experimental.pallas import tpu as pltpu
from jax.sharding import PartitionSpec as P

LANES = 128
SUB = 8
VMEM = pl.BlockSpec(memory_space=pltpu.VMEM)
HBM = pl.BlockSpec(memory_space=pltpu.HBM)
SMEM = pl.BlockSpec(memory_space=pltpu.SMEM)
USUAL = 52


def halves(x):
    high = x.astype(jnp.bfloat16)
    low = (x - high.astype(jnp.float32)).astype(jnp.bfloat16)
    return high, low


def spread(
    groups, mine, depth, rows, tiles,
    src_hbm, cnt_hbm, irr_hbm, row_hbm, amp_hbm, out_ref, place_ref,
    src_ref, cnt_ref, irr_ref, row_ref, amp_ref, sems,
):
    pairs = [
        (amp_hbm, amp_ref), (irr_hbm, irr_ref), (src_hbm, src_ref), (cnt_hbm, cnt_ref),
        (row_hbm, row_ref),
    ]
    copies = [pltpu.make_async_copy(a, b, sems.at[n]) for n, (a, b) in enumerate(pairs)]
    for copy in copies:
        copy.start()
    me = lax.axis_index("col")
    share = rows // groups
    chunk = share * mine + SUB
    before = lax.broadcasted_iota(jnp.int32, (tiles, tiles), 0)
    after = lax.broadcasted_iota(jnp.int32, (tiles, tiles), 1)
    earlier = jnp.where(before < after, 1.0, 0.0).astype(jnp.bfloat16)
    for copy in copies[1:]:
        copy.wait()
    tile = lax.broadcasted_iota(jnp.int32, (1, tiles), 1)
    label = row_ref[...] * tiles + tile
    listed = jnp.zeros((1, tiles), jnp.int32)
    for m in range(mine):
        base = irr_ref[me * mine + m] * tiles
        count = cnt_ref[m]
        for k in range(depth):
            key = jnp.where(k < count, src_ref[m, k] + base, -1)
            listed = jnp.where(label == key, 1, listed)
    owned = (tile >= me * mine) & (tile < me * mine + mine)
    listed = jnp.where(owned, 0, listed)
    rank = jnp.dot(
        jnp.broadcast_to(listed, (2 * SUB, tiles)).astype(jnp.float32).astype(jnp.bfloat16),
        earlier,
        preferred_element_type=jnp.float32,
    )[:1]
    place = jnp.where(listed > 0, rank, -1.0)
    place_ref[...] = place.astype(jnp.int32)
    line = lax.broadcasted_iota(jnp.int32, (SUB, LANES), 0)
    sheet = jnp.zeros((SUB, LANES), jnp.float32)
    for n in range(tiles // LANES):
        sheet = jnp.where(line == n, place[:, n * LANES : (n + 1) * LANES], sheet)
    for j in range(groups):
        out_ref[pl.ds(j * chunk + share * mine, SUB), :] = sheet
    copies[0].wait()
    for i in range(rows // SUB):
        r, j = divmod(i * SUB, groups)
        for m in range(mine):
            out_ref[pl.ds(j * chunk + r * mine + m, SUB, stride=chunk), :] = amp_ref[
                pl.ds(i * SUB, SUB), pl.ds(m * LANES, LANES)
            ]


def pick(groups, mine, slots, usual, share, tiles, got_ref, out_ref, rest_ref, more_ref, hot_ref):
    chunk = share * mine + SUB
    table = jnp.concatenate(
        [
            jnp.concatenate(
                [got_ref[pl.ds(g * chunk + r * mine, mine), :] for g in range(groups)], axis=0
            )
            for r in range(share)
        ],
        axis=1,
    )
    high, low = halves(table)
    both = jnp.concatenate([high, low], axis=1)
    last = got_ref[pl.ds(share * mine, groups, stride=chunk), :]
    for n in range(1, tiles // LANES):
        last = jnp.maximum(last, got_ref[pl.ds(share * mine + n, groups, stride=chunk), :])
    more_ref[0] = (jnp.max(last) >= usual).astype(jnp.int32)
    at = lax.broadcasted_iota(jnp.int32, (slots, tiles), 0).astype(jnp.float32)
    for g in range(groups):
        place = jnp.concatenate(
            [got_ref[pl.ds(g * chunk + share * mine + n, 1), :] for n in range(tiles // LANES)],
            axis=1,
        )
        hot_ref[pl.ds(g * slots, slots), :] = jnp.where(at == place, 1.0, 0.0).astype(jnp.bfloat16)
    width = share * LANES
    step = 512
    for b in range(groups * slots // step):
        sums = jnp.dot(
            hot_ref[pl.ds(b * step, step), :], both, preferred_element_type=jnp.float32
        )
        sums = sums[:, :width] + sums[:, width:]
        for g in range(step // slots):
            to = (b * step // slots + g) * share
            for r in range(share):
                mid = g * slots + usual
                lanes = slice(r * LANES, (r + 1) * LANES)
                out_ref[pl.ds((to + r) * usual, usual), :] = sums[g * slots : mid, lanes]
                rest_ref[pl.ds((to + r) * (slots - usual), slots - usual), :] = sums[
                    mid : (g + 1) * slots, lanes
                ]


def multiply(
    late, groups, half, mine, depth, rows, usual,
    par_hbm, src_hbm, cnt_hbm, irr_hbm, place_hbm, extra_ref, got_ref, int_ref, out_ref, turned_ref,
    par_ref, src_ref, cnt_ref, irr_ref, place_ref, term_ref, sems,
):
    pairs = [
        (src_hbm, src_ref), (cnt_hbm, cnt_ref), (irr_hbm, irr_ref), (place_hbm, place_ref),
        (par_hbm, par_ref),
    ]
    copies = [pltpu.make_async_copy(a, b, sems.at[n]) for n, (a, b) in enumerate(pairs)]
    for copy in copies:
        copy.start()
    share = rows // groups
    first = lax.axis_index("col") * mine
    other_first = lax.rem(lax.axis_index("col") + half, groups) * mine
    step = depth * LANES
    for m in range(mine):
        at = pl.ds(m * step, step)
        term_ref[at, :] = jnp.concatenate(halves(int_ref[at, :]), axis=1)
    for copy in copies:
        copy.wait()
    low, count = (usual, mine * depth - usual) if late else (0, usual)
    for m in range(mine):
        cols = []
        for k in range(depth):
            source = src_ref[m, k]
            place = place_ref[0, source]
            live = (k < cnt_ref[m]) & (irr_ref[source] == irr_ref[first + m])
            at = jnp.clip(place - low, 0, count - 1)
            block = jnp.concatenate(
                [
                    got_ref[pl.ds(r * count + at, groups, stride=share * count), :]
                    for r in range(share)
                ],
                axis=0,
            )
            if late:
                live = live & (place >= usual)
            else:
                live = live & (place < usual)
                owned = (source >= first) & (source < first + mine)
                own = jnp.where(owned, source - first, 0)
                own_block = extra_ref[:, pl.ds(pl.multiple_of(own * LANES, LANES), LANES)]
                block = jnp.where(owned, own_block, block)
            cols.append(jnp.where(live, block, 0.0))
        left_high, left_low = halves(jnp.concatenate(cols, axis=1))
        sums = jnp.dot(
            jnp.concatenate([left_high, left_low], axis=0),
            term_ref[pl.ds(m * step, step), :],
            preferred_element_type=jnp.float32,
        )
        sums = sums[:, :LANES] + sums[:, LANES:]
        sums = sums[:rows] + sums[rows:]
        if late:
            sums = sums + extra_ref[m]
        out_ref[m] = sums
        turned_ref[par_ref[first + m] - other_first] = sums


def finish(mine, rows, lad_ref, mir_ref, occ_ref, virt_ref, out_ref):
    row = lax.broadcasted_iota(jnp.int32, (rows, rows), 0)
    col = lax.broadcasted_iota(jnp.int32, (rows, rows), 1)
    occ = jnp.sum(jnp.where(row == col, occ_ref[...], 0.0), axis=1, keepdims=True)
    for m in range(mine):
        lanes = pl.ds(m * LANES, LANES)
        out_ref[:, lanes] = (lad_ref[m] + mir_ref[m]) / (occ - virt_ref[:, lanes])


def shards(amplitudes, integrals, sources, counts, tile_irrep, partner, occ_energy, virt_energy):
    rows = amplitudes.shape[0]
    mine, depth, width, _ = integrals.shape
    tiles = tile_irrep.shape[0]
    cols = lax.axis_size("col")
    heights = lax.axis_size("row")
    slots = mine * depth
    share = rows // cols
    chunk = share * mine + SUB
    f32 = jnp.float32

    i32 = jnp.int32
    usual = USUAL
    left = slots - usual

    def call(body, out, *args, specs, outs=None, scratch=(), flops=0, moved=0, room=16):
        return pl.pallas_call(
            body,
            out_shape=[jax.ShapeDtypeStruct(shape, dtype) for shape, dtype in out],
            in_specs=specs,
            out_specs=outs or [VMEM] * len(out),
            scratch_shapes=scratch,
            compiler_params=pltpu.CompilerParams(vmem_limit_bytes=room * 1024 * 1024),
            cost_estimate=pl.CostEstimate(flops=flops, bytes_accessed=moved, transcendentals=0),
        )(*args)

    sent, place = call(
        lambda *refs: spread(cols, mine, depth, rows, tiles, *refs),
        [((cols * chunk, LANES), f32), ((1, tiles), i32)],
        sources, counts, tile_irrep, tile_irrep.reshape(1, tiles), amplitudes,
        specs=[HBM] * 5,
        scratch=[
            pltpu.SMEM(sources.shape, i32),
            pltpu.SMEM(counts.shape, i32),
            pltpu.SMEM((tiles,), i32),
            pltpu.VMEM((1, tiles), i32),
            pltpu.VMEM(amplitudes.shape, f32),
            pltpu.SemaphoreType.DMA((5,)),
        ],
        moved=2 * amplitudes.size * 4,
        room=63,
    )
    got = lax.all_to_all(sent.reshape(cols, chunk, LANES), "col", 0, 0)
    sent, rest, more = call(
        lambda *refs: pick(cols, mine, slots, usual, share, tiles, *refs),
        [
            ((cols * share * usual, LANES), f32),
            ((cols * share * left, LANES), f32),
            ((1,), i32),
        ],
        got.reshape(cols * chunk, LANES),
        specs=[VMEM],
        outs=[VMEM, VMEM, SMEM],
        scratch=[pltpu.VMEM((cols * slots, tiles), jnp.bfloat16)],
        flops=4 * cols * slots * tiles * share * LANES,
        moved=cols * slots * share * LANES * 4,
    )
    got = lax.all_to_all(sent.reshape(cols, share * usual, LANES), "col", 0, 0)

    def products(late, extra, got):
        return call(
            lambda *refs: multiply(late, cols, cols // 2, mine, depth, rows, usual, *refs),
            [((mine, rows, width), f32)] * 2,
            partner, sources, counts, tile_irrep, place, extra, got.reshape(-1, LANES),
            integrals.reshape(mine * depth * width, width),
            specs=[HBM] * 5 + [VMEM] * 3,
            scratch=[
                pltpu.SMEM((tiles,), i32),
                pltpu.SMEM(sources.shape, i32),
                pltpu.SMEM(counts.shape, i32),
                pltpu.SMEM((tiles,), i32),
                pltpu.SMEM((1, tiles), i32),
                pltpu.VMEM((mine * depth * width, 2 * width), jnp.bfloat16),
                pltpu.SemaphoreType.DMA((5,)),
            ],
            flops=8 * rows * mine * depth * width * width,
            moved=integrals.size * 4 + got.size * 4,
        )

    pairs = [
        (r * cols + c, (r + heights // 2) % heights * cols + (c + cols // 2) % cols)
        for r in range(heights)
        for c in range(cols)
    ]

    def close(ladder, mirrored, rest):
        return call(
            lambda *refs: finish(mine, rows, *refs),
            [((rows, mine * width), f32)],
            ladder, mirrored, occ_energy.reshape(1, rows),
            virt_energy.reshape(1, mine * width),
            specs=[VMEM] * 4,
            moved=4 * rows * mine * width * 3,
        )[0]

    def amend(ladder, mirrored, rest):
        rest = lax.all_to_all(rest.reshape(cols, share * left, LANES), "col", 0, 0)
        ladder, turned = products(True, ladder, rest)
        return close(ladder, lax.ppermute(turned, ("row", "col"), pairs), rest)

    ladder, turned = products(False, amplitudes, got)
    more, turned = lax.optimization_barrier((more, turned))
    mirrored = lax.ppermute(turned, ("row", "col"), pairs)
    return lax.cond(more[0] > 0, amend, close, ladder, mirrored, rest)


def solution(mesh):
    placed = (
        P("row", "col"),
        P("col", None, None, None),
        P("col", None),
        P("col"),
        P(),
        P(),
        P("row"),
        P("col"),
    )
    return jax.shard_map(
        shards, mesh=mesh, in_specs=placed, out_specs=P("row", "col"), check_vma=False
    )
```

time: 70.8 us -> 66.4 us (0.938)
  blocking collectives: 49 us -> 44.7 us
  waiting for transfers between devices: 9.67 us -> 8.57 us
  local copies, waits for them, and re-layouts: 0.02 us -> 0.75 us
  between operations: 0.05 us -> 0.78 us
    all_to_all x1, blocking collectives: 30.9 us -> 26.6 us  [shards(): got = lax.all_to_all(sent.reshape(cols, share * usual, LANES), 'col', 0, 0)]
    ppermute x1, waiting for transfers between devices: 9.67 us -> 8.57 us  [shards(): mirrored = lax.ppermute(turned, ('row', 'col'), pairs)]
    unnamed x8 -> x18, local copies, waits for them, and re-layouts: 0.02 us -> 0.75 us
where the time goes in v3:
time: 66.4 us; the launch traced here: 66.2 us
  blocking collectives  44.7 us (67%)
  waiting for transfers between devices  8.57 us (13%)
  starting transfers between devices  6.28 us (9%)
  Pallas kernels  5.11 us (8%)
  between operations  0.78 us (1%)
  local copies, waits for them, and re-layouts  0.75 us (1%)
    all_to_all x1, blocking collectives, shards(): got = lax.all_to_all(sent.reshape(cols, share * usual, LANES), 'col', 0, 0)  26.6 us
    all_to_all x1, blocking collectives, shards(): got = lax.all_to_all(sent.reshape(cols, chunk, LANES), 'col', 0, 0)  18.1 us
    ppermute x1, waiting for transfers between devices, shards(): mirrored = lax.ppermute(turned, ('row', 'col'), pairs)  8.57 us
    ppermute x1, starting transfers between devices, shards(): mirrored = lax.ppermute(turned, ('row', 'col'), pairs)  6.28 us
    pallas_call x4, Pallas kernels, call(): pl.pallas_call(body, out_shape=[jax.ShapeDtypeStruct(shape, dtype) for sh...  5.11 us
  transfers between devices with their start and end apart: 1, of which 1 were waited for; matrix products, arithmetic and copies ran while one was open for 0% of the time, Pallas kernels for 0%

profile of v3, /device:TPU:2, one launch (start us, length us, event | category | flops | bytes accessed | tf_op | source)
XLA Modules:
  0.0 66.2 jit_solution(11374997310198577703)
XLA Ops:
  0.0 1.9 %shard_map.84 = (f32[768,128]{1,0:T(8,128)}, s32[1,256]{1,0:T(1,128)S(1)}) custom-call(s32[8,8]{1,0:T(8,128)} %refs_1_.3, s32[8]{0:T(128)} %refs_2_.3, s32[256]{0:T(256)} %refs_3_.1, s32[1,256]{1,0:T(1,128)} %bitcast.24, f32[64,1024]{1,0:T(8,128)} %refs_5_.1), custom_call_target="tpu_custom_call" | custom-call | bytes 524288 | tf_op jit(solution)/shard_map/pallas_call | solution.py:201
  1.9 18.1 %all_to_all.15 = f32[32,24,128]{2,1,0:T(8,128)S(1)} all-to-all(f32[32,24,128]{2,1,0:T(8,128)} %bitcast.21), channel_id=1, replica_groups=mesh['row'=8,'col'=32] {'col'}, dimensions={0} | all-to-all | bytes 786432 | tf_op jit(solution)/shard_map/all_to_all | solution.py:227
  20.0 1.2 %shard_map.85 = (f32[3328,128]{1,0:T(8,128)S(1)}, f32[768,128]{1,0:T(8,128)S(1)}, s32[1]{0:T(128)}) custom-call(f32[768,128]{1,0:T(8,128)S(1)} %bitcast.17), custom_call_target="tpu_custom_call" | custom-call | flops 536870912 | bytes 2097152 | tf_op jit(solution)/shard_map/pallas_call | solution.py:201
  21.2 0.0 copy-start
  21.2 0.0 copy-start.3
  21.2 0.0 copy-start.5
  21.2 0.0 copy-start.6
  21.2 0.0 copy-start.7
  21.2 26.6 %all_to_all.16 = f32[32,104,128]{2,1,0:T(8,128)S(1)} all-to-all(f32[32,104,128]{2,1,0:T(8,128)S(1)} %bitcast.15), channel_id=1, replica_groups=mesh['row'=8,'col'=32] {'col'}, dimensions={0} | all-to-all | bytes 3407872 | tf_op jit(solution)/shard_map/all_to_all | solution.py:242
  47.8 0.0 copy-done.1
  47.8 0.0 copy-done
  47.9 0.0 copy-done.3
  47.9 0.0 copy-done.5
  47.9 0.0 copy-done.6
  47.9 0.0 copy-start.4
  47.9 0.0 copy-start.8
  47.9 1.9 %shard_map.86 = (f32[8,64,128]{2,1,0:T(8,128)S(1)}, f32[8,64,128]{2,1,0:T(8,128)S(1)}) custom-call(s32[256]{0:T(256)S(1)} %copy-done.7, s32[8,8]{1,0:T(8,128)S(1)} %copy-done.3, s32[8]{0:T(128)S(1)} %copy-done.6, s32[256]{0:T(256)S(1)} %copy-done.5, s32[1,256]{1,0:T(1,128)S(1)} %get-tuple-element.63.refs_4_, f32[64,1024]{1,0:T(8,128)S(1)} %copy-done, ...), custom_call_target="tpu_custom_call" | custom-call | flops 536870912 | bytes 5898240 | tf_op jit(solution)/shard_map/pallas_call | solution.py:201
  49.8 6.3 %collective-permute-start.1 = (f32[8,64,128]{2,1,0:T(8,128)S(1)}, f32[8,64,128]{2,1,0:T(8,128)S(1)}, u32[]{:S(2)}, u32[]{:S(2)}) collective-permute-start(f32[8,64,128]{2,1,0:T(8,128)S(1)} %get-tuple-element.68), channel_id=1, source_target_pairs={{0,144},{1,145},{2,146},{3,147},{4,148},{5,149},{6,150},{7,151},{8... | collective-permute-start | bytes 786440 | tf_op jit(solution)/shard_map/ppermute | solution.py:287
  56.8 8.6 %collective-permute-done.1 = f32[8,64,128]{2,1,0:T(8,128)S(1)} collective-permute-done((f32[8,64,128]{2,1,0:T(8,128)S(1)}, f32[8,64,128]{2,1,0:T(8,128)S(1)}, u32[]{:S(2)}, u32[]{:S(2)}) %collective-permute-start.1) | collective-permute-done | bytes 262176 | tf_op jit(solution)/shard_map/ppermute | solution.py:287
  65.3 0.0 copy-done.8
  65.3 0.1 conditional.1
  65.3 0.1 branch_0_fun.1
  65.5 0.0 copy-start.2
  65.5 0.7 %copy-done.2 = f32[64,1024]{1,0:T(8,128)} copy-done((f32[64,1024]{1,0:T(8,128)}, f32[64,1024]{1,0:T(8,128)S(1)}, u32[]{:S(2)}) %copy-start.2) | copy-done | bytes 262168
  (3 shorter events, 0.0 us)
Async XLA Ops:
  20.0 27.9 %copy-start.1 = (f32[8,8,128,128]{3,2,1,0:T(8,128)S(1)}, f32[8,8,128,128]{3,2,1,0:T(8,128)}, u32[]{:S(2)}) copy-start(f32[8,8,128,128]{3,2,1,0:T(8,128)} %param.11) | copy-start | bytes 12582916
  21.2 26.7 %copy-start = (f32[64,1024]{1,0:T(8,128)S(1)}, f32[64,1024]{1,0:T(8,128)}, u32[]{:S(2)}) copy-start(f32[64,1024]{1,0:T(8,128)} %refs_5_.1) | copy-start | bytes 786436
  21.2 26.7 %copy-start.3 = (s32[8,8]{1,0:T(8,128)S(1)}, s32[8,8]{1,0:T(8,128)}, u32[]{:S(2)}) copy-start(s32[8,8]{1,0:T(8,128)} %refs_1_.3) | copy-start | bytes 772
  21.2 26.7 %copy-start.5 = (s32[256]{0:T(256)S(1)}, s32[256]{0:T(256)}, u32[]{:S(2)}) copy-start(s32[256]{0:T(256)} %refs_3_.1) | copy-start | bytes 3076
  21.2 26.7 %copy-start.6 = (s32[8]{0:T(128)S(1)}, s32[8]{0:T(128)}, u32[]{:S(2)}) copy-start(s32[8]{0:T(128)} %refs_2_.3) | copy-start | bytes 100
  21.2 26.7 %copy-start.7 = (s32[256]{0:T(256)S(1)}, s32[256]{0:T(256)}, u32[]{:S(2)}) copy-start(s32[256]{0:T(256)} %refs_0_.3) | copy-start | bytes 3076
  47.9 17.4 %copy-start.4 = (f32[1024]{0:T(1024)S(1)}, f32[1024]{0:T(1024)}, u32[]{:S(2)}) copy-start(f32[1024]{0:T(1024)} %param.17) | copy-start | bytes 12292
  47.9 17.4 %copy-start.8 = (f32[64]{0:T(128)S(1)}, f32[64]{0:T(128)}, u32[]{:S(2)}) copy-start(f32[64]{0:T(128)} %param.16) | copy-start | bytes 772
  49.8 15.5 %collective-permute-start.1 = (f32[8,64,128]{2,1,0:T(8,128)S(1)}, f32[8,64,128]{2,1,0:T(8,128)S(1)}, u32[]{:S(2)}, u32[]{:S(2)}) collective-permute-start(f32[8,64,128]{2,1,0:T(8,128)S(1)} %get-tuple-element.68), channel_id=1, source_target_pairs={{0,144},{1,145},{2,146},{3,147},{4,148},{5,149},{6,150},{7,151},{8... | collective-permute-start | bytes 786440 | tf_op jit(solution)/shard_map/ppermute | solution.py:287
  65.5 0.7 %copy-start.2 = (f32[64,1024]{1,0:T(8,128)}, f32[64,1024]{1,0:T(8,128)S(1)}, u32[]{:S(2)}) copy-start(f32[64,1024]{1,0:T(8,128)S(1)} %get-tuple-element.77) | copy-start | bytes 786436

commit v4 on v3

--- a/solution.py
+++ b/solution.py
@@ -10,7 +10,7 @@
 VMEM = pl.BlockSpec(memory_space=pltpu.VMEM)
 HBM = pl.BlockSpec(memory_space=pltpu.HBM)
 SMEM = pl.BlockSpec(memory_space=pltpu.SMEM)
-USUAL = 52
+USUAL = 55
 
 
 def halves(x):
@@ -33,7 +33,7 @@
         copy.start()
     me = lax.axis_index("col")
     share = rows // groups
-    chunk = share * mine + SUB
+    chunk = share * mine + tiles // LANES
     before = lax.broadcasted_iota(jnp.int32, (tiles, tiles), 0)
     after = lax.broadcasted_iota(jnp.int32, (tiles, tiles), 1)
     earlier = jnp.where(before < after, 1.0, 0.0).astype(jnp.bfloat16)
@@ -62,7 +62,7 @@
     for n in range(tiles // LANES):
         sheet = jnp.where(line == n, place[:, n * LANES : (n + 1) * LANES], sheet)
     for j in range(groups):
-        out_ref[pl.ds(j * chunk + share * mine, SUB), :] = sheet
+        out_ref[pl.ds(j * chunk + share * mine, tiles // LANES), :] = sheet[: tiles // LANES]
     copies[0].wait()
     for i in range(rows // SUB):
         r, j = divmod(i * SUB, groups)
@@ -73,7 +73,7 @@
 
 
 def pick(groups, mine, slots, usual, share, tiles, got_ref, out_ref, rest_ref, more_ref, hot_ref):
-    chunk = share * mine + SUB
+    chunk = share * mine + tiles // LANES
     table = jnp.concatenate(
         [
             jnp.concatenate(
@@ -190,7 +190,7 @@
     heights = lax.axis_size("row")
     slots = mine * depth
     share = rows // cols
-    chunk = share * mine + SUB
+    chunk = share * mine + tiles // LANES
     f32 = jnp.float32
 
     i32 = jnp.int32
@@ -224,7 +224,7 @@
         moved=2 * amplitudes.size * 4,
         room=63,
     )
-    got = lax.all_to_all(sent.reshape(cols, chunk, LANES), "col", 0, 0)
+    got = lax.all_to_all(sent.reshape(cols, chunk, 1, LANES), "col", 0, 0)
     sent, rest, more = call(
         lambda *refs: pick(cols, mine, slots, usual, share, tiles, *refs),
         [
@@ -239,7 +239,7 @@
         flops=4 * cols * slots * tiles * share * LANES,
         moved=cols * slots * share * LANES * 4,
     )
-    got = lax.all_to_all(sent.reshape(cols, share * usual, LANES), "col", 0, 0)
+    got = lax.all_to_all(sent.reshape(cols, share * usual, 1, LANES), "col", 0, 0)
 
     def products(late, extra, got):
         return call(
@@ -278,7 +278,7 @@
         )[0]
 
     def amend(ladder, mirrored, rest):
-        rest = lax.all_to_all(rest.reshape(cols, share * left, LANES), "col", 0, 0)
+        rest = lax.all_to_all(rest.reshape(cols, share * left, 1, LANES), "col", 0, 0)
         ladder, turned = products(True, ladder, rest)
         return close(ladder, lax.ppermute(turned, ("row", "col"), pairs), rest)
 

time: 66.4 us -> 66.3 us (level)
  no operation moved by 1% of the time
where the time goes in v4:
time: 66.3 us; the launch traced here: 66.1 us
  blocking collectives  44.9 us (68%)
  waiting for transfers between devices  8.44 us (13%)
  starting transfers between devices  6.35 us (10%)
  Pallas kernels  4.81 us (7%)
  between operations  0.78 us (1%)
  local copies, waits for them, and re-layouts  0.75 us (1%)
    all_to_all x1, blocking collectives, shards(): lax.all_to_all(sent.reshape(cols, share * usual, 1, LANES), 'col', 0, 0)  27.8 us
    all_to_all x1, blocking collectives, shards(): got = lax.all_to_all(sent.reshape(cols, chunk, 1, LANES), 'col', 0, 0)  17.1 us
    ppermute x1, waiting for transfers between devices, shards(): mirrored = lax.ppermute(turned, ('row', 'col'), pairs)  8.44 us
    ppermute x1, starting transfers between devices, shards(): mirrored = lax.ppermute(turned, ('row', 'col'), pairs)  6.35 us
    pallas_call x4, Pallas kernels, call(): pl.pallas_call(body, out_shape=[jax.ShapeDtypeStruct(shape, dtype) for sh...  4.81 us
  transfers between devices with their start and end apart: 1, of which 1 were waited for; matrix products, arithmetic and copies ran while one was open for 0% of the time, Pallas kernels for 0%

profile of v4, /device:TPU:2, one launch (start us, length us, event | category | flops | bytes accessed | tf_op | source)
XLA Modules:
  0.0 66.1 jit_solution(605241494632104876)
XLA Ops:
  0.0 1.9 %shard_map.84 = (f32[576,128]{1,0:T(8,128)}, s32[1,256]{1,0:T(1,128)S(1)}) custom-call(s32[8,8]{1,0:T(8,128)} %refs_1_.3, s32[8]{0:T(128)} %refs_2_.3, s32[256]{0:T(256)} %refs_3_.1, s32[1,256]{1,0:T(1,128)} %bitcast.24, f32[64,1024]{1,0:T(8,128)} %refs_5_.1), custom_call_target="tpu_custom_call" | custom-call | bytes 524288 | tf_op jit(solution)/shard_map/pallas_call | solution.py:201
  1.9 17.1 %all_to_all.15 = f32[32,18,1,128]{3,2,1,0:T(1,128)S(1)} all-to-all(f32[32,18,1,128]{3,2,1,0:T(1,128)} %bitcast.21), channel_id=1, replica_groups=mesh['row'=8,'col'=32] {'col'}, dimensions={0} | all-to-all | bytes 589824 | tf_op jit(solution)/shard_map/all_to_all | solution.py:227
  19.0 1.2 %shard_map.85 = (f32[3520,128]{1,0:T(8,128)S(1)}, f32[576,128]{1,0:T(8,128)S(1)}, s32[1]{0:T(128)}) custom-call(f32[576,128]{1,0:T(8,128)S(1)} %bitcast.17), custom_call_target="tpu_custom_call" | custom-call | flops 536870912 | bytes 2097152 | tf_op jit(solution)/shard_map/pallas_call | solution.py:201
  20.2 0.0 copy-start
  20.2 0.0 copy-start.3
  20.2 0.0 copy-start.5
  20.2 0.0 copy-start.6
  20.2 0.0 copy-start.7
  20.2 27.8 %all_to_all.16 = f32[32,110,1,128]{3,2,1,0:T(1,128)S(1)} all-to-all(f32[32,110,1,128]{3,2,1,0:T(1,128)S(1)} %bitcast.15), channel_id=1, replica_groups=mesh['row'=8,'col'=32] {'col'}, dimensions={0} | all-to-all | bytes 3604480 | tf_op jit(solution)/shard_map/all_to_all | solution.py:242
  48.0 0.0 copy-done.1
  48.0 0.0 copy-done
  48.0 0.0 copy-done.3
  48.0 0.0 copy-done.5
  48.0 0.0 copy-done.6
  48.1 0.0 copy-start.4
  48.1 0.0 copy-start.8
  48.1 1.7 %shard_map.86 = (f32[8,64,128]{2,1,0:T(8,128)S(1)}, f32[8,64,128]{2,1,0:T(8,128)S(1)}) custom-call(s32[256]{0:T(256)S(1)} %copy-done.7, s32[8,8]{1,0:T(8,128)S(1)} %copy-done.3, s32[8]{0:T(128)S(1)} %copy-done.6, s32[256]{0:T(256)S(1)} %copy-done.5, s32[1,256]{1,0:T(1,128)S(1)} %get-tuple-element.63.refs_4_, f32[64,1024]{1,0:T(8,128)S(1)} %copy-done, ...), custom_call_target="tpu_custom_call" | custom-call | flops 536870912 | bytes 5996544 | tf_op jit(solution)/shard_map/pallas_call | solution.py:201
  49.8 6.4 %collective-permute-start.1 = (f32[8,64,128]{2,1,0:T(8,128)S(1)}, f32[8,64,128]{2,1,0:T(8,128)S(1)}, u32[]{:S(2)}, u32[]{:S(2)}) collective-permute-start(f32[8,64,128]{2,1,0:T(8,128)S(1)} %get-tuple-element.68), channel_id=1, source_target_pairs={{0,144},{1,145},{2,146},{3,147},{4,148},{5,149},{6,150},{7,151},{8... | collective-permute-start | bytes 786440 | tf_op jit(solution)/shard_map/ppermute | solution.py:287
  56.8 8.4 %collective-permute-done.1 = f32[8,64,128]{2,1,0:T(8,128)S(1)} collective-permute-done((f32[8,64,128]{2,1,0:T(8,128)S(1)}, f32[8,64,128]{2,1,0:T(8,128)S(1)}, u32[]{:S(2)}, u32[]{:S(2)}) %collective-permute-start.1) | collective-permute-done | bytes 262176 | tf_op jit(solution)/shard_map/ppermute | solution.py:287
  65.2 0.0 copy-done.8
  65.2 0.1 conditional.1
  65.2 0.1 branch_0_fun.1
  65.4 0.0 copy-start.2
  65.4 0.7 %copy-done.2 = f32[64,1024]{1,0:T(8,128)} copy-done((f32[64,1024]{1,0:T(8,128)}, f32[64,1024]{1,0:T(8,128)S(1)}, u32[]{:S(2)}) %copy-start.2) | copy-done | bytes 262168
  (3 shorter events, 0.0 us)
Async XLA Ops:
  19.0 29.0 %copy-start.1 = (f32[8,8,128,128]{3,2,1,0:T(8,128)S(1)}, f32[8,8,128,128]{3,2,1,0:T(8,128)}, u32[]{:S(2)}) copy-start(f32[8,8,128,128]{3,2,1,0:T(8,128)} %param.11) | copy-start | bytes 12582916
  20.2 27.9 %copy-start = (f32[64,1024]{1,0:T(8,128)S(1)}, f32[64,1024]{1,0:T(8,128)}, u32[]{:S(2)}) copy-start(f32[64,1024]{1,0:T(8,128)} %refs_5_.1) | copy-start | bytes 786436
  20.2 27.8 %copy-start.3 = (s32[8,8]{1,0:T(8,128)S(1)}, s32[8,8]{1,0:T(8,128)}, u32[]{:S(2)}) copy-start(s32[8,8]{1,0:T(8,128)} %refs_1_.3) | copy-start | bytes 772
  20.2 27.8 %copy-start.5 = (s32[256]{0:T(256)S(1)}, s32[256]{0:T(256)}, u32[]{:S(2)}) copy-start(s32[256]{0:T(256)} %refs_3_.1) | copy-start | bytes 3076
  20.2 27.8 %copy-start.6 = (s32[8]{0:T(128)S(1)}, s32[8]{0:T(128)}, u32[]{:S(2)}) copy-start(s32[8]{0:T(128)} %refs_2_.3) | copy-start | bytes 100
  20.2 27.8 %copy-start.7 = (s32[256]{0:T(256)S(1)}, s32[256]{0:T(256)}, u32[]{:S(2)}) copy-start(s32[256]{0:T(256)} %refs_0_.3) | copy-start | bytes 3076
  48.1 17.2 %copy-start.4 = (f32[1024]{0:T(1024)S(1)}, f32[1024]{0:T(1024)}, u32[]{:S(2)}) copy-start(f32[1024]{0:T(1024)} %param.17) | copy-start | bytes 12292
  48.1 17.2 %copy-start.8 = (f32[64]{0:T(128)S(1)}, f32[64]{0:T(128)}, u32[]{:S(2)}) copy-start(f32[64]{0:T(128)} %param.16) | copy-start | bytes 772
  49.8 15.4 %collective-permute-start.1 = (f32[8,64,128]{2,1,0:T(8,128)S(1)}, f32[8,64,128]{2,1,0:T(8,128)S(1)}, u32[]{:S(2)}, u32[]{:S(2)}) collective-permute-start(f32[8,64,128]{2,1,0:T(8,128)S(1)} %get-tuple-element.68), channel_id=1, source_target_pairs={{0,144},{1,145},{2,146},{3,147},{4,148},{5,149},{6,150},{7,151},{8... | collective-permute-start | bytes 786440 | tf_op jit(solution)/shard_map/ppermute | solution.py:287
  65.4 0.7 %copy-start.2 = (f32[64,1024]{1,0:T(8,128)}, f32[64,1024]{1,0:T(8,128)S(1)}, u32[]{:S(2)}) copy-start(f32[64,1024]{1,0:T(8,128)S(1)} %get-tuple-element.77) | copy-start | bytes 786436

commit v5 on v4

--- a/solution.py
+++ b/solution.py
@@ -25,8 +25,8 @@
     src_ref, cnt_ref, irr_ref, row_ref, amp_ref, sems,
 ):
     pairs = [
-        (amp_hbm, amp_ref), (irr_hbm, irr_ref), (src_hbm, src_ref), (cnt_hbm, cnt_ref),
-        (row_hbm, row_ref),
+        (irr_hbm, irr_ref), (src_hbm, src_ref), (cnt_hbm, cnt_ref), (row_hbm, row_ref),
+        (amp_hbm, amp_ref),
     ]
     copies = [pltpu.make_async_copy(a, b, sems.at[n]) for n, (a, b) in enumerate(pairs)]
     for copy in copies:
@@ -37,7 +37,7 @@
     before = lax.broadcasted_iota(jnp.int32, (tiles, tiles), 0)
     after = lax.broadcasted_iota(jnp.int32, (tiles, tiles), 1)
     earlier = jnp.where(before < after, 1.0, 0.0).astype(jnp.bfloat16)
-    for copy in copies[1:]:
+    for copy in copies[:4]:
         copy.wait()
     tile = lax.broadcasted_iota(jnp.int32, (1, tiles), 1)
     label = row_ref[...] * tiles + tile
@@ -63,7 +63,7 @@
         sheet = jnp.where(line == n, place[:, n * LANES : (n + 1) * LANES], sheet)
     for j in range(groups):
         out_ref[pl.ds(j * chunk + share * mine, tiles // LANES), :] = sheet[: tiles // LANES]
-    copies[0].wait()
+    copies[4].wait()
     for i in range(rows // SUB):
         r, j = divmod(i * SUB, groups)
         for m in range(mine):

time: 66.3 us -> 66.2 us (level)
  no operation moved by 1% of the time
where the time goes in v5:
time: 66.2 us; the launch traced here: 65.9 us
  blocking collectives  44.9 us (68%)
  waiting for transfers between devices  8.44 us (13%)
  starting transfers between devices  6.36 us (10%)
  Pallas kernels  4.69 us (7%)
  between operations  0.78 us (1%)
  local copies, waits for them, and re-layouts  0.75 us (1%)
    all_to_all x1, blocking collectives, shards(): lax.all_to_all(sent.reshape(cols, share * usual, 1, LANES), 'col', 0, 0)  27.8 us
    all_to_all x1, blocking collectives, shards(): got = lax.all_to_all(sent.reshape(cols, chunk, 1, LANES), 'col', 0, 0)  17.1 us
    ppermute x1, waiting for transfers between devices, shards(): mirrored = lax.ppermute(turned, ('row', 'col'), pairs)  8.44 us
    ppermute x1, starting transfers between devices, shards(): mirrored = lax.ppermute(turned, ('row', 'col'), pairs)  6.36 us
    pallas_call x4, Pallas kernels, call(): pl.pallas_call(body, out_shape=[jax.ShapeDtypeStruct(shape, dtype) for sh...  4.69 us
  transfers between devices with their start and end apart: 1, of which 1 were waited for; matrix products, arithmetic and copies ran while one was open for 0% of the time, Pallas kernels for 0%

profile of v5, /device:TPU:2, one launch (start us, length us, event | category | flops | bytes accessed | tf_op | source)
XLA Modules:
  0.0 65.9 jit_solution(7322930511435034785)
XLA Ops:
  0.0 1.7 %shard_map.84 = (f32[576,128]{1,0:T(8,128)}, s32[1,256]{1,0:T(1,128)S(1)}) custom-call(s32[8,8]{1,0:T(8,128)} %refs_1_.3, s32[8]{0:T(128)} %refs_2_.3, s32[256]{0:T(256)} %refs_3_.1, s32[1,256]{1,0:T(1,128)} %bitcast.24, f32[64,1024]{1,0:T(8,128)} %refs_5_.1), custom_call_target="tpu_custom_call" | custom-call | bytes 524288 | tf_op jit(solution)/shard_map/pallas_call | solution.py:201
  1.7 17.1 %all_to_all.15 = f32[32,18,1,128]{3,2,1,0:T(1,128)S(1)} all-to-all(f32[32,18,1,128]{3,2,1,0:T(1,128)} %bitcast.21), channel_id=1, replica_groups=mesh['row'=8,'col'=32] {'col'}, dimensions={0} | all-to-all | bytes 589824 | tf_op jit(solution)/shard_map/all_to_all | solution.py:227
  18.9 1.2 %shard_map.85 = (f32[3520,128]{1,0:T(8,128)S(1)}, f32[576,128]{1,0:T(8,128)S(1)}, s32[1]{0:T(128)}) custom-call(f32[576,128]{1,0:T(8,128)S(1)} %bitcast.17), custom_call_target="tpu_custom_call" | custom-call | flops 536870912 | bytes 2097152 | tf_op jit(solution)/shard_map/pallas_call | solution.py:201
  20.0 0.0 copy-start
  20.1 0.0 copy-start.3
  20.1 0.0 copy-start.5
  20.1 0.0 copy-start.6
  20.1 0.0 copy-start.7
  20.1 27.8 %all_to_all.16 = f32[32,110,1,128]{3,2,1,0:T(1,128)S(1)} all-to-all(f32[32,110,1,128]{3,2,1,0:T(1,128)S(1)} %bitcast.15), channel_id=1, replica_groups=mesh['row'=8,'col'=32] {'col'}, dimensions={0} | all-to-all | bytes 3604480 | tf_op jit(solution)/shard_map/all_to_all | solution.py:242
  47.9 0.0 copy-done.1
  47.9 0.0 copy-done
  47.9 0.0 copy-done.3
  47.9 0.0 copy-done.5
  47.9 0.0 copy-done.6
  47.9 0.0 copy-done.7
  47.9 0.0 copy-start.4
  47.9 0.0 copy-start.8
  48.0 1.7 %shard_map.86 = (f32[8,64,128]{2,1,0:T(8,128)S(1)}, f32[8,64,128]{2,1,0:T(8,128)S(1)}) custom-call(s32[256]{0:T(256)S(1)} %copy-done.7, s32[8,8]{1,0:T(8,128)S(1)} %copy-done.3, s32[8]{0:T(128)S(1)} %copy-done.6, s32[256]{0:T(256)S(1)} %copy-done.5, s32[1,256]{1,0:T(1,128)S(1)} %get-tuple-element.63.refs_4_, f32[64,1024]{1,0:T(8,128)S(1)} %copy-done, ...), custom_call_target="tpu_custom_call" | custom-call | flops 536870912 | bytes 5996544 | tf_op jit(solution)/shard_map/pallas_call | solution.py:201
  49.6 6.4 %collective-permute-start.1 = (f32[8,64,128]{2,1,0:T(8,128)S(1)}, f32[8,64,128]{2,1,0:T(8,128)S(1)}, u32[]{:S(2)}, u32[]{:S(2)}) collective-permute-start(f32[8,64,128]{2,1,0:T(8,128)S(1)} %get-tuple-element.68), channel_id=1, source_target_pairs={{0,144},{1,145},{2,146},{3,147},{4,148},{5,149},{6,150},{7,151},{8... | collective-permute-start | bytes 786440 | tf_op jit(solution)/shard_map/ppermute | solution.py:287
  56.7 8.4 %collective-permute-done.1 = f32[8,64,128]{2,1,0:T(8,128)S(1)} collective-permute-done((f32[8,64,128]{2,1,0:T(8,128)S(1)}, f32[8,64,128]{2,1,0:T(8,128)S(1)}, u32[]{:S(2)}, u32[]{:S(2)}) %collective-permute-start.1) | collective-permute-done | bytes 262176 | tf_op jit(solution)/shard_map/ppermute | solution.py:287
  65.1 0.1 conditional.1
  65.1 0.1 branch_0_fun.1
  65.2 0.0 copy-start.2
  65.2 0.7 %copy-done.2 = f32[64,1024]{1,0:T(8,128)} copy-done((f32[64,1024]{1,0:T(8,128)}, f32[64,1024]{1,0:T(8,128)S(1)}, u32[]{:S(2)}) %copy-start.2) | copy-done | bytes 262168
  (3 shorter events, 0.0 us)
Async XLA Ops:
  18.9 29.0 %copy-start.1 = (f32[8,8,128,128]{3,2,1,0:T(8,128)S(1)}, f32[8,8,128,128]{3,2,1,0:T(8,128)}, u32[]{:S(2)}) copy-start(f32[8,8,128,128]{3,2,1,0:T(8,128)} %param.11) | copy-start | bytes 12582916
  20.0 27.9 %copy-start = (f32[64,1024]{1,0:T(8,128)S(1)}, f32[64,1024]{1,0:T(8,128)}, u32[]{:S(2)}) copy-start(f32[64,1024]{1,0:T(8,128)} %refs_5_.1) | copy-start | bytes 786436
  20.1 27.8 %copy-start.3 = (s32[8,8]{1,0:T(8,128)S(1)}, s32[8,8]{1,0:T(8,128)}, u32[]{:S(2)}) copy-start(s32[8,8]{1,0:T(8,128)} %refs_1_.3) | copy-start | bytes 772
  20.1 27.8 %copy-start.5 = (s32[256]{0:T(256)S(1)}, s32[256]{0:T(256)}, u32[]{:S(2)}) copy-start(s32[256]{0:T(256)} %refs_3_.1) | copy-start | bytes 3076
  20.1 27.8 %copy-start.6 = (s32[8]{0:T(128)S(1)}, s32[8]{0:T(128)}, u32[]{:S(2)}) copy-start(s32[8]{0:T(128)} %refs_2_.3) | copy-start | bytes 100
  20.1 27.8 %copy-start.7 = (s32[256]{0:T(256)S(1)}, s32[256]{0:T(256)}, u32[]{:S(2)}) copy-start(s32[256]{0:T(256)} %refs_0_.3) | copy-start | bytes 3076
  47.9 17.2 %copy-start.4 = (f32[1024]{0:T(1024)S(1)}, f32[1024]{0:T(1024)}, u32[]{:S(2)}) copy-start(f32[1024]{0:T(1024)} %param.17) | copy-start | bytes 12292
  47.9 17.2 %copy-start.8 = (f32[64]{0:T(128)S(1)}, f32[64]{0:T(128)}, u32[]{:S(2)}) copy-start(f32[64]{0:T(128)} %param.16) | copy-start | bytes 772
  49.6 15.4 %collective-permute-start.1 = (f32[8,64,128]{2,1,0:T(8,128)S(1)}, f32[8,64,128]{2,1,0:T(8,128)S(1)}, u32[]{:S(2)}, u32[]{:S(2)}) collective-permute-start(f32[8,64,128]{2,1,0:T(8,128)S(1)} %get-tuple-element.68), channel_id=1, source_target_pairs={{0,144},{1,145},{2,146},{3,147},{4,148},{5,149},{6,150},{7,151},{8... | collective-permute-start | bytes 786440 | tf_op jit(solution)/shard_map/ppermute | solution.py:287
  65.2 0.7 %copy-start.2 = (f32[64,1024]{1,0:T(8,128)}, f32[64,1024]{1,0:T(8,128)S(1)}, u32[]{:S(2)}) copy-start(f32[64,1024]{1,0:T(8,128)S(1)} %get-tuple-element.77) | copy-start | bytes 786436

commit v6 on v5

--- a/solution.py
+++ b/solution.py
@@ -1,3 +1,5 @@
+import functools
+
 import jax
 import jax.numpy as jnp
 from jax import lax
@@ -88,7 +90,8 @@
     last = got_ref[pl.ds(share * mine, groups, stride=chunk), :]
     for n in range(1, tiles // LANES):
         last = jnp.maximum(last, got_ref[pl.ds(share * mine + n, groups, stride=chunk), :])
-    more_ref[0] = (jnp.max(last) >= usual).astype(jnp.int32)
+    more = jnp.max(last) >= usual
+    more_ref[0] = more.astype(jnp.int32)
     at = lax.broadcasted_iota(jnp.int32, (slots, tiles), 0).astype(jnp.float32)
     for g in range(groups):
         place = jnp.concatenate(
@@ -103,15 +106,16 @@
             hot_ref[pl.ds(b * step, step), :], both, preferred_element_type=jnp.float32
         )
         sums = sums[:, :width] + sums[:, width:]
-        for g in range(step // slots):
-            to = (b * step // slots + g) * share
-            for r in range(share):
-                mid = g * slots + usual
-                lanes = slice(r * LANES, (r + 1) * LANES)
-                out_ref[pl.ds((to + r) * usual, usual), :] = sums[g * slots : mid, lanes]
-                rest_ref[pl.ds((to + r) * (slots - usual), slots - usual), :] = sums[
-                    mid : (g + 1) * slots, lanes
-                ]
+        def keep(ref, low, high):
+            for g in range(step // slots):
+                to = (b * step // slots + g) * share
+                for r in range(share):
+                    ref[pl.ds((to + r) * (high - low), high - low), :] = sums[
+                        g * slots + low : g * slots + high, r * LANES : (r + 1) * LANES
+                    ]
+
+        keep(out_ref, 0, usual)
+        pl.when(more)(functools.partial(keep, rest_ref, usual, slots))
 
 
 def multiply(

time: 66.2 us -> 67.3 us (1.017)
  Pallas kernels: 4.69 us -> 5.84 us
    pallas_call x4, Pallas kernels: 4.69 us -> 5.84 us  [call(): pl.pallas_call(body, out_shape=[jax.ShapeDtypeStruct(shape, dtype) for sh...]
where the time goes in v6:
time: 67.3 us; the launch traced here: 67.1 us
  blocking collectives  44.9 us (67%)
  waiting for transfers between devices  8.44 us (13%)
  starting transfers between devices  6.37 us (9%)
  Pallas kernels  5.84 us (9%)
  between operations  0.78 us (1%)
  local copies, waits for them, and re-layouts  0.75 us (1%)
    all_to_all x1, blocking collectives, shards(): lax.all_to_all(sent.reshape(cols, share * usual, 1, LANES), 'col', 0, 0)  27.8 us
    all_to_all x1, blocking collectives, shards(): got = lax.all_to_all(sent.reshape(cols, chunk, 1, LANES), 'col', 0, 0)  17.1 us
    ppermute x1, waiting for transfers between devices, shards(): mirrored = lax.ppermute(turned, ('row', 'col'), pairs)  8.44 us
    ppermute x1, starting transfers between devices, shards(): mirrored = lax.ppermute(turned, ('row', 'col'), pairs)  6.37 us
    pallas_call x4, Pallas kernels, call(): pl.pallas_call(body, out_shape=[jax.ShapeDtypeStruct(shape, dtype) for sh...  5.84 us
  transfers between devices with their start and end apart: 1, of which 1 were waited for; matrix products, arithmetic and copies ran while one was open for 0% of the time, Pallas kernels for 0%

profile of v6, /device:TPU:2, one launch (start us, length us, event | category | flops | bytes accessed | tf_op | source)
XLA Modules:
  0.0 67.1 jit_solution(2826603847017419620)
XLA Ops:
  0.0 1.7 %shard_map.84 = (f32[576,128]{1,0:T(8,128)}, s32[1,256]{1,0:T(1,128)S(1)}) custom-call(s32[8,8]{1,0:T(8,128)} %refs_1_.3, s32[8]{0:T(128)} %refs_2_.3, s32[256]{0:T(256)} %refs_3_.1, s32[1,256]{1,0:T(1,128)} %bitcast.24, f32[64,1024]{1,0:T(8,128)} %refs_5_.1), custom_call_target="tpu_custom_call" | custom-call | bytes 524288 | tf_op jit(solution)/shard_map/pallas_call | solution.py:205
  1.7 17.1 %all_to_all.15 = f32[32,18,1,128]{3,2,1,0:T(1,128)S(1)} all-to-all(f32[32,18,1,128]{3,2,1,0:T(1,128)} %bitcast.21), channel_id=1, replica_groups=mesh['row'=8,'col'=32] {'col'}, dimensions={0} | all-to-all | bytes 589824 | tf_op jit(solution)/shard_map/all_to_all | solution.py:231
  18.9 2.3 %shard_map.85 = (f32[3520,128]{1,0:T(8,128)S(1)}, f32[576,128]{1,0:T(8,128)S(1)}, s32[1]{0:T(128)}) custom-call(f32[576,128]{1,0:T(8,128)S(1)} %bitcast.17), custom_call_target="tpu_custom_call" | custom-call | flops 536870912 | bytes 2097152 | tf_op jit(solution)/shard_map/pallas_call | solution.py:205
  21.2 0.0 copy-start
  21.2 0.0 copy-start.3
  21.2 0.0 copy-start.5
  21.2 0.0 copy-start.6
  21.2 0.0 copy-start.7
  21.3 27.8 %all_to_all.16 = f32[32,110,1,128]{3,2,1,0:T(1,128)S(1)} all-to-all(f32[32,110,1,128]{3,2,1,0:T(1,128)S(1)} %bitcast.15), channel_id=1, replica_groups=mesh['row'=8,'col'=32] {'col'}, dimensions={0} | all-to-all | bytes 3604480 | tf_op jit(solution)/shard_map/all_to_all | solution.py:246
  49.0 0.0 copy-done.1
  49.0 0.0 copy-done
  49.0 0.0 copy-done.3
  49.1 0.0 copy-done.5
  49.1 0.0 copy-done.6
  49.1 0.0 copy-start.4
  49.1 0.0 copy-start.8
  49.1 1.7 %shard_map.86 = (f32[8,64,128]{2,1,0:T(8,128)S(1)}, f32[8,64,128]{2,1,0:T(8,128)S(1)}) custom-call(s32[256]{0:T(256)S(1)} %copy-done.7, s32[8,8]{1,0:T(8,128)S(1)} %copy-done.3, s32[8]{0:T(128)S(1)} %copy-done.6, s32[256]{0:T(256)S(1)} %copy-done.5, s32[1,256]{1,0:T(1,128)S(1)} %get-tuple-element.63.refs_4_, f32[64,1024]{1,0:T(8,128)S(1)} %copy-done, ...), custom_call_target="tpu_custom_call" | custom-call | flops 536870912 | bytes 5996544 | tf_op jit(solution)/shard_map/pallas_call | solution.py:205
  50.8 6.4 %collective-permute-start.1 = (f32[8,64,128]{2,1,0:T(8,128)S(1)}, f32[8,64,128]{2,1,0:T(8,128)S(1)}, u32[]{:S(2)}, u32[]{:S(2)}) collective-permute-start(f32[8,64,128]{2,1,0:T(8,128)S(1)} %get-tuple-element.68), channel_id=1, source_target_pairs={{0,144},{1,145},{2,146},{3,147},{4,148},{5,149},{6,150},{7,151},{8... | collective-permute-start | bytes 786440 | tf_op jit(solution)/shard_map/ppermute | solution.py:291
  57.8 8.4 %collective-permute-done.1 = f32[8,64,128]{2,1,0:T(8,128)S(1)} collective-permute-done((f32[8,64,128]{2,1,0:T(8,128)S(1)}, f32[8,64,128]{2,1,0:T(8,128)S(1)}, u32[]{:S(2)}, u32[]{:S(2)}) %collective-permute-start.1) | collective-permute-done | bytes 262176 | tf_op jit(solution)/shard_map/ppermute | solution.py:291
  66.3 0.0 copy-done.4
  66.3 0.1 conditional.1
  66.3 0.1 branch_0_fun.1
  66.4 0.0 copy-start.2
  66.4 0.7 %copy-done.2 = f32[64,1024]{1,0:T(8,128)} copy-done((f32[64,1024]{1,0:T(8,128)}, f32[64,1024]{1,0:T(8,128)S(1)}, u32[]{:S(2)}) %copy-start.2) | copy-done | bytes 262168
  (3 shorter events, 0.0 us)
Async XLA Ops:
  18.9 30.2 %copy-start.1 = (f32[8,8,128,128]{3,2,1,0:T(8,128)S(1)}, f32[8,8,128,128]{3,2,1,0:T(8,128)}, u32[]{:S(2)}) copy-start(f32[8,8,128,128]{3,2,1,0:T(8,128)} %param.11) | copy-start | bytes 12582916
  21.2 27.9 %copy-start = (f32[64,1024]{1,0:T(8,128)S(1)}, f32[64,1024]{1,0:T(8,128)}, u32[]{:S(2)}) copy-start(f32[64,1024]{1,0:T(8,128)} %refs_5_.1) | copy-start | bytes 786436
  21.2 27.8 %copy-start.3 = (s32[8,8]{1,0:T(8,128)S(1)}, s32[8,8]{1,0:T(8,128)}, u32[]{:S(2)}) copy-start(s32[8,8]{1,0:T(8,128)} %refs_1_.3) | copy-start | bytes 772
  21.2 27.8 %copy-start.5 = (s32[256]{0:T(256)S(1)}, s32[256]{0:T(256)}, u32[]{:S(2)}) copy-start(s32[256]{0:T(256)} %refs_3_.1) | copy-start | bytes 3076
  21.2 27.8 %copy-start.6 = (s32[8]{0:T(128)S(1)}, s32[8]{0:T(128)}, u32[]{:S(2)}) copy-start(s32[8]{0:T(128)} %refs_2_.3) | copy-start | bytes 100
  21.2 27.8 %copy-start.7 = (s32[256]{0:T(256)S(1)}, s32[256]{0:T(256)}, u32[]{:S(2)}) copy-start(s32[256]{0:T(256)} %refs_0_.3) | copy-start | bytes 3076
  49.1 17.2 %copy-start.4 = (f32[1024]{0:T(1024)S(1)}, f32[1024]{0:T(1024)}, u32[]{:S(2)}) copy-start(f32[1024]{0:T(1024)} %param.17) | copy-start | bytes 12292
  49.1 17.2 %copy-start.8 = (f32[64]{0:T(128)S(1)}, f32[64]{0:T(128)}, u32[]{:S(2)}) copy-start(f32[64]{0:T(128)} %param.16) | copy-start | bytes 772
  50.8 15.5 %collective-permute-start.1 = (f32[8,64,128]{2,1,0:T(8,128)S(1)}, f32[8,64,128]{2,1,0:T(8,128)S(1)}, u32[]{:S(2)}, u32[]{:S(2)}) collective-permute-start(f32[8,64,128]{2,1,0:T(8,128)S(1)} %get-tuple-element.68), channel_id=1, source_target_pairs={{0,144},{1,145},{2,146},{3,147},{4,148},{5,149},{6,150},{7,151},{8... | collective-permute-start | bytes 786440 | tf_op jit(solution)/shard_map/ppermute | solution.py:291
  66.4 0.7 %copy-start.2 = (f32[64,1024]{1,0:T(8,128)}, f32[64,1024]{1,0:T(8,128)S(1)}, u32[]{:S(2)}) copy-start(f32[64,1024]{1,0:T(8,128)S(1)} %get-tuple-element.77) | copy-start | bytes 786436
